TPU v7x, 512 devices: a whole 4x4x16 slice. The times are simulated.
512 devices in a mesh: dp: 32 (over z_hi, y, core), tensor: 16 (over z_lo, x).
Axes of the slice: x: 4, y: 4, z: 16 (z_hi: 4, z_lo: 4; z = z_hi * 4 + z_lo), core: 2. Of those that a mesh axis runs over, the one named last changes fastest.
Arguments:
- attention: bfloat16 [8192, 4096], P('dp', 'tensor'), may hold values from -6 to 6
- residual: bfloat16 [8192, 4096], P(('dp', 'tensor'))
- out_weight: bfloat16 [4096, 4096], P('tensor'), may hold values from -0.09375 to 0.09375
- norm_gain: float32 [4096], replicated, may hold values from 0.1 to 1.9
- grad_normed: bfloat16 [8192, 4096], P(('dp', 'tensor'))
- grad_resid: bfloat16 [8192, 4096], P(('dp', 'tensor')), may hold values from -6 to 6
Outputs:
- normed: bfloat16 [8192, 4096], P(('dp', 'tensor'))
- stream_out: bfloat16 [8192, 4096], P(('dp', 'tensor'))
- stream_grad: bfloat16 [8192, 4096], P(('dp', 'tensor'))
- attn_grad: bfloat16 [8192, 4096], P('dp', 'tensor')
- weight_grad: float32 [4096, 4096], P('tensor', 'dp')
- gain_grad: float32 [4096], replicated
All inputs are finite; a program needn't handle non-finite values.
Results may differ from a plain program's by a relative error of at most 0.02.
Values may be sent and summed in bfloat16 or wider, within the bound.
No kernel may reach another device: no remote copies, remote signals or barrier semaphores. Data moves between devices by JAX's collectives and lax.ppermute only.
A program may use at most 64 MiB of HBM per device.

v0:
```python
import jax
import jax.numpy as jnp
from jax import lax
from jax.sharding import PartitionSpec as P


def local(attention, residual, out_weight, norm_gain, grad_normed, grad_resid):
    projected = lax.psum_scatter(
        jnp.dot(attention, out_weight, preferred_element_type=jnp.float32).astype(jnp.bfloat16),
        "tensor",
        scatter_dimension=0,
        tiled=True,
    ).astype(jnp.float32)
    stream_out = (residual.astype(jnp.float32) + projected).astype(jnp.bfloat16)
    values = stream_out.astype(jnp.float32)
    inv_rms = lax.rsqrt(jnp.mean(values * values, axis=-1, keepdims=True) + 1e-05)
    unit_rows = values * inv_rms
    normed = (unit_rows * norm_gain).astype(jnp.bfloat16)
    upstream = grad_normed.astype(jnp.float32)
    gain_grad = lax.psum(jnp.sum(upstream * unit_rows, axis=0), ("dp", "tensor"))
    scaled_grad = upstream * norm_gain
    inner = jnp.mean(scaled_grad * unit_rows, axis=-1, keepdims=True)
    stream_grad = (
        grad_resid.astype(jnp.float32) + inv_rms * (scaled_grad - unit_rows * inner)
    ).astype(jnp.bfloat16)
    block_grads = lax.all_gather(stream_grad, "tensor", axis=0, tiled=True)
    attn_grad = lax.dot_general(
        block_grads, out_weight, (((1,), (1,)), ((), ())), preferred_element_type=jnp.float32
    ).astype(jnp.bfloat16)
    local_grad = lax.dot_general(
        attention, block_grads, (((0,), (0,)), ((), ())), preferred_element_type=jnp.float32
    )
    weight_grad = lax.psum_scatter(
        local_grad.astype(jnp.bfloat16), "dp", scatter_dimension=1, tiled=True
    ).astype(jnp.float32)
    return (normed, stream_out, stream_grad, attn_grad, weight_grad, gain_grad)


def solution(mesh):
    return jax.shard_map(
        local,
        mesh=mesh,
        in_specs=(
            P("dp", "tensor"),
            P(("dp", "tensor"), None),
            P("tensor", None),
            P(),
            P(("dp", "tensor"), None),
            P(("dp", "tensor"), None),
        ),
        out_specs=(
            P(("dp", "tensor"), None),
            P(("dp", "tensor"), None),
            P(("dp", "tensor"), None),
            P("dp", "tensor"),
            P("tensor", "dp"),
            P(),
        ),
        check_vma=False,
    )
```

profile of v0, /device:TPU:6, one launch (start us, length us, event | category | flops | bytes accessed | tf_op | source)
XLA Modules:
  0.0 328.8 jit_solution(12454239115942249782)
XLA Ops:
  7.2 0.0 copy-start
  7.2 0.0 reduce-scatter.3.cloned.1.call-start
  7.2 1.5 copy-done
  8.8 3.0 convolution_convert_fusion.1
  11.7 0.0 copy-start.4
  11.7 0.0 copy-start.3
  11.7 0.0 copy-start.6
  11.7 0.0 copy-start.5
  11.7 0.0 copy-start.2
  11.7 0.0 reduce-scatter.3.cloned.1.call-update
  11.8 0.0 all-gather.2.cloned.1.call-start
  11.8 88.7 %reduce-scatter.3.cloned.1.call-done = bf16[16,4096]{1,0:T(8,128)(2,1)} async-done(((bf16[256,4096]{1,0:T(8,128)(2,1)}), bf16[16,4096]{1,0:T(8,128)(2,1)}) %reduce-scatter.3.cloned.1.call-update) | async-done | bytes 131088 | tf_op jit(solution)/shard_map/reduce_scatter | solution.py:8
  100.6 0.0 copy-done.4
  100.6 1.1 fusion.10
  101.6 0.0 copy-start.1
  101.6 0.0 copy-done.3
  101.7 0.0 copy-done.6
  101.7 0.3 fusion.11
  102.0 0.0 copy-done.5
  102.0 0.9 fusion.7
  102.8 0.0 all-gather.2.cloned.1.call-update
  102.9 0.0 reduce-scatter.5.cloned.1.call-start
  102.9 89.0 %all-gather.2.cloned.1.call-done = bf16[256,4096]{1,0:T(8,128)(2,1)} async-done(((bf16[16,4096]{1,0:T(8,128)(2,1)}), bf16[256,4096]{1,0:T(8,128)(2,1)}) %all-gather.2.cloned.1.call-update) | async-done | bytes 2097168 | tf_op jit(solution)/shard_map/all_gather | solution.py:26
  191.9 0.0 copy-done.2
  191.9 3.7 %fusion = bf16[256,4096]{0,1:T(8,128)(2,1)} fusion(bf16[256,4096]{1,0:T(8,128)(2,1)} %all-gather.2.cloned.1.call-done, bf16[256,256]{1,0:T(8,128)(2,1)S(1)} %copy-done.2), kind=kOutput, calls=%fused_computation.2 | convolution fusion | flops 537919488 | bytes 4325376 | tf_op jit(solution)/shard_map/dot_general | solution.py:30
  195.6 0.0 copy-done.1
  195.6 0.0 reduce-scatter.5.cloned.1.call-update
  195.6 114.7 %psum.7 = f32[4096]{0:T(1024)} all-reduce(f32[4096]{0:T(1024)S(1)} %get-tuple-element.12), channel_id=1, replica_groups=mesh['dp'=32,'tensor'=16] {'dp','tensor'}, use_global_device_ids=true, to_apply=%region_5.0 | all-reduce | flops 4096 | bytes 32768 | tf_op jit(solution)/shard_map/psum | solution.py:20
  310.3 3.0 convolution_convert_fusion.2
  313.3 7.4 %reduce-scatter.5.cloned.1.call-done = bf16[256,128]{0,1:T(8,128)(2,1)} async-done(((bf16[256,4096]{0,1:T(8,128)(2,1)}), bf16[256,128]{0,1:T(8,128)(2,1)}) %reduce-scatter.5.cloned.1.call-update) | async-done | bytes 65552 | tf_op jit(solution)/shard_map/reduce_scatter | solution.py:33
  320.7 1.6 copy.12
  (2 shorter events, 0.0 us)
Async XLA Ops:
  7.2 1.6 copy-start
  7.2 93.4 %reduce-scatter.3.cloned.1.call-start = ((), (), s32[]{:S(2)}) async-start(), calls=%async_computation.2 | async-start | bytes 2228224 | tf_op jit(solution)/shard_map/reduce_scatter | solution.py:8
  11.7 88.8 %copy-start.4 = (bf16[16,4096]{1,0:T(8,128)(2,1)S(1)}, bf16[16,4096]{1,0:T(8,128)(2,1)}, u32[]{:S(2)}) copy-start(bf16[16,4096]{1,0:T(8,128)(2,1)} %param.7) | copy-start | bytes 393220
  11.7 89.9 %copy-start.3 = (bf16[16,4096]{1,0:T(8,128)(2,1)S(1)}, bf16[16,4096]{1,0:T(8,128)(2,1)}, u32[]{:S(2)}) copy-start(bf16[16,4096]{1,0:T(8,128)(2,1)} %param.10) | copy-start | bytes 393220
  11.7 89.9 %copy-start.6 = (f32[4096]{0:T(1024)S(1)}, f32[4096]{0:T(1024)}, u32[]{:S(2)}) copy-start(f32[4096]{0:T(1024)} %param.9) | copy-start | bytes 49156
  11.7 90.2 %copy-start.5 = (bf16[16,4096]{1,0:T(8,128)(2,1)S(1)}, bf16[16,4096]{1,0:T(8,128)(2,1)}, u32[]{:S(2)}) copy-start(bf16[16,4096]{1,0:T(8,128)(2,1)} %param.11) | copy-start | bytes 393220
  11.7 180.2 %copy-start.2 = (bf16[256,256]{1,0:T(8,128)(2,1)S(1)}, bf16[256,256]{1,0:T(8,128)(2,1)}, u32[]{:S(2)}) copy-start(bf16[256,256]{1,0:T(8,128)(2,1)} %param.6) | copy-start | bytes 393220
  11.8 180.1 %all-gather.2.cloned.1.call-start = ((), (), s32[]{:S(2)}) async-start(), calls=%async_computation.3 | async-start | bytes 2228224 | tf_op jit(solution)/shard_map/all_gather | solution.py:26
  101.6 93.9 %copy-start.1 = (bf16[16,4096]{1,0:T(8,128)(2,1)}, bf16[16,4096]{1,0:T(8,128)(2,1)S(1)}, u32[]{:S(2)}) copy-start(bf16[16,4096]{1,0:T(8,128)(2,1)S(1)} %get-tuple-element.15) | copy-start | bytes 393220
  102.9 217.8 %reduce-scatter.5.cloned.1.call-start = ((), (), s32[]{:S(2)}) async-start(), calls=%async_computation.4 | async-start | bytes 2162688 | tf_op jit(solution)/shard_map/reduce_scatter | solution.py:33
Sparse Core Ops, SparseCore 0:
  11.9 88.6 reduce-scatter.2
  103.2 88.6 all-gather.1
  196.3 124.3 reduce-scatter.4
where the time goes:
time: 329 us
  waiting for transfers between devices  185 us (56%)
  blocking collectives  115 us (35%)
  between operations  13.8 us (4%)
  matrix products  9.6 us (3%)
    psum x1, blocking collectives, local(): lax.psum(jnp.sum(upstream * unit_rows, axis=0), ('dp', 'tensor'))  115 us
    all_gather x1, waiting for transfers between devices, local(): block_grads = lax.all_gather(stream_grad, 'tensor', axis=0, tiled=True)  89 us
    reduce_scatter x1, waiting for transfers between devices, local(): lax.psum_scatter(jnp.dot(attention, out_weight, preferred_element_type=jn...  88.7 us
    reduce_scatter x1, waiting for transfers between devices, local(): lax.psum_scatter(local_grad.astype(jnp.bfloat16), 'dp', scatter_dimension...  7.37 us
  transfers between devices with their start and end apart: 3, of which 3 were waited for; matrix products, arithmetic and copies ran while one was open for 1% of the time, Pallas kernels for 0%

commit v1 on v0

v1 whole, which is shorter than its diff:
```python
import jax
import jax.numpy as jnp
from jax import lax
from jax.experimental import pallas as pl
from jax.experimental.pallas import tpu as pltpu
from jax.sharding import Mesh, PartitionSpec as P

BF16, F32 = jnp.bfloat16, jnp.float32
AXES = ("zh", "y", "c", "zl", "x")
PARAMS = pltpu.CompilerParams(vmem_limit_bytes=48 * 2**20)
SCALAR = pl.BlockSpec(memory_space=pltpu.SMEM)
WHOLE = pl.BlockSpec(memory_space=pltpu.VMEM)


def shape(dims, dtype=BF16):
    return jax.ShapeDtypeStruct(dims, dtype)


def call(kernel, out_shape, *args):
    specs = [SCALAR if a.dtype == jnp.int32 else WHOLE for a in args]
    return pl.pallas_call(kernel, out_shape=out_shape, in_specs=specs, compiler_params=PARAMS)(*args)


def a2a(value, axes):
    return lax.all_to_all(value, axes, 0, 0, tiled=True)


def ring(step):
    return [(i, (i + step) % 4) for i in range(4)]


def forward_kernel(yc_ref, att_ref, weight_ref, out_ref, cols_ref):
    att = jnp.concatenate(
        [att_ref[z * 64 + x * 16 : z * 64 + x * 16 + 16] for x in range(4) for z in range(4)]
    )
    out_ref[...] = jnp.dot(att, weight_ref[...], preferred_element_type=F32).astype(BF16)
    for h in range(4):
        start = pl.multiple_of(yc_ref[0] * 128 + h * 1024, 128)
        cols_ref[:, h * 128 : h * 128 + 128] = weight_ref[:, pl.ds(start, 128)]


def norm_kernel(
    parts_ref, residual_ref, gain_ref, upstream_ref, resid_grad_ref,
    normed_ref, stream_ref, grad_ref, cols_ref, gain_grad_ref,
):
    projected = parts_ref[0].astype(F32)
    for k in range(1, 4):
        projected += parts_ref[k].astype(F32)
    stream_out = (residual_ref[...].astype(F32) + projected).astype(BF16)
    stream_ref[...] = stream_out
    values = stream_out.astype(F32)
    inv_rms = lax.rsqrt(jnp.mean(values * values, axis=-1, keepdims=True) + 1e-05)
    unit_rows = values * inv_rms
    gain = gain_ref[...]
    normed_ref[...] = (unit_rows * gain).astype(BF16)
    upstream = upstream_ref[...].astype(F32)
    gain_grad = jnp.sum(upstream * unit_rows, axis=0, keepdims=True)
    scaled = upstream * gain
    inner = jnp.mean(scaled * unit_rows, axis=-1, keepdims=True)
    grad = (resid_grad_ref[...].astype(F32) + inv_rms * (scaled - unit_rows * inner)).astype(BF16)
    grad_ref[...] = grad
    for c in range(2):
        for y in range(4):
            for h in range(4):
                start = (h * 8 + y * 2 + c) * 128
                for z in range(4):
                    to = (c * 4 + y) * 4 + z
                    cols_ref[to, :, h * 128 : h * 128 + 128] = grad[:, start : start + 128]
                    gain_grad_ref[to, :, h * 128 : h * 128 + 128] = gain_grad[:, start : start + 128]


def weight_kernel(at_ref, gain_ref, att_ref, *refs):
    x, zh = at_ref[0], at_ref[1]
    total = jnp.zeros((256, 512), F32)
    for piece_ref, step in zip(refs[:4], (0, 3, 1, 2)):
        att = att_ref[:, :, lax.rem(x + step, 4)].reshape(512, 256)
        total += lax.dot_general(
            att, piece_ref[...], (((0,), (0,)), ((), ())), preferred_element_type=F32
        )
    refs[8][...] = total
    gain = gain_ref[...]
    upper = gain.astype(BF16)
    lower = (gain - upper.astype(F32)).astype(BF16)
    for j in range(4):
        start = pl.multiple_of(lax.rem(zh + j, 4) * 128, 128)
        refs[4 + j][:256] = refs[8][:, pl.ds(start, 128)].astype(BF16)
        refs[4 + j][256:288] = upper
        refs[4 + j][288:] = lower


def weight_sum_kernel(*refs):
    total = refs[0][...].astype(F32)
    for ref in refs[1:4]:
        total += ref[...].astype(F32)
    refs[4][...] = total[:256]
    refs[5][...] = total[256:288] + total[288:]


def back_kernel(at_ref, weight_ref, *refs):
    for piece_ref, step in zip(refs[:4], (0, 3, 1, 2)):
        rows = lax.dot_general(
            piece_ref[...], weight_ref[...], (((1,), (1,)), ((), ())), preferred_element_type=F32
        )
        refs[4][:, :, lax.rem(at_ref[0] + step, 4)] = rows.reshape(8, 4, 16, 256).astype(BF16)


def local(attention, residual, out_weight, norm_gain, grad_normed, grad_resid):
    zh, x, y, c = (lax.axis_index(n).astype(jnp.int32) for n in ("zh", "x", "y", "c"))
    at = jnp.stack([x, zh, c])

    partial, weight_cols = call(
        forward_kernel,
        (shape((256, 4096)), shape((256, 512))),
        (y * 2 + c).reshape(1),
        attention,
        out_weight,
    )
    att_all = lax.all_gather(attention, ("c", "y"), axis=0, tiled=True)
    by_x = a2a(partial, "x").reshape(4, 64, 4096)
    sum_x = jnp.sum(by_x.astype(F32), axis=0).astype(BF16)
    by_z = a2a(sum_x, "zl").reshape(4, 16, 4096)
    by_z, att_all = lax.optimization_barrier((by_z, att_all))

    normed, stream_out, stream_grad, cols, gain = call(
        norm_kernel,
        (shape((16, 4096)),) * 3 + (shape((32, 16, 512)), shape((32, 1, 512), F32)),
        by_z,
        residual,
        norm_gain.reshape(1, 4096),
        grad_normed,
        grad_resid,
    )

    grads = a2a(cols, ("c", "y", "zl")).reshape(512, 512)
    grads, gain = lax.optimization_barrier((grads, gain))
    pieces = [grads] + [lax.ppermute(grads, "x", ring(k)) for k in (1, 3, 2)]

    gain = jnp.sum(a2a(gain, ("c", "y", "zl")), axis=0, keepdims=True)
    gain = a2a(jnp.broadcast_to(gain, (32, 1, 512)), ("c", "y", "x"))
    gain = jnp.sum(gain.reshape(8, 4, 4, 128), axis=1).reshape(32, 128)

    blocks = pl.pallas_call(
        weight_kernel,
        out_shape=(shape((320, 128)),) * 4,
        in_specs=[SCALAR] + [WHOLE] * 6,
        scratch_shapes=[pltpu.VMEM((256, 512), F32)],
        compiler_params=PARAMS,
    )(at, gain, att_all.reshape(8, 4, 4, 16, 256), *pieces)
    moved = [lax.ppermute(blocks[k], "zh", ring(k)) for k in (1, 3, 2)]
    weight_grad, gain = call(
        weight_sum_kernel, (shape((256, 128), F32), shape((32, 128), F32)), blocks[0], *moved
    )
    gain_grad = gain.reshape(2, 4, 4, 128).transpose(2, 1, 0, 3).reshape(4096)

    weight_cols, _ = lax.optimization_barrier((weight_cols, blocks[0]))
    back = call(back_kernel, shape((8, 4, 4, 16, 256)), at, weight_cols, *pieces)
    back = back.reshape(8, 256, 256)
    attn_grad = lax.psum_scatter(back, ("c", "y"), scatter_dimension=0, tiled=True).reshape(256, 256)
    return (normed, stream_out, stream_grad, attn_grad, weight_grad, gain_grad)


def solution(mesh):
    fine = Mesh(mesh.devices.reshape(4, 4, 2, 4, 4), AXES)
    dp, tensor = ("zh", "y", "c"), ("zl", "x")
    rows = P(dp + tensor, None)
    return jax.shard_map(
        local,
        mesh=fine,
        in_specs=(P(dp, tensor), rows, P(tensor, None), P(), rows, rows),
        out_specs=(rows, rows, rows, P(dp, tensor), P(tensor, dp), P()),
        check_vma=False,
    )
```

time: 329 us -> 174 us (0.53)
  waiting for transfers between devices: 185 us -> 63.5 us
  blocking collectives: 115 us -> 22.1 us
  starting transfers between devices: 0.12 us -> 59.2 us
  matrix products: 9.6 us -> 0 us
  Pallas kernels: 0 us -> 7.48 us
    psum x1 -> x0, blocking collectives: 115 us -> none  [local(): lax.psum(jnp.sum(upstream * unit_rows, axis=0), ('dp', 'tensor'))]
    reduce_scatter x2 -> x1, waiting for transfers between devices: 96.1 us -> 12.5 us  [local(): lax.psum_scatter(back, ('c', 'y'), scatter_dimension=0, tiled=True)]
    all_gather x1, waiting for transfers between devices: 89 us -> 7.09 us  [local(): att_all = lax.all_gather(attention, ('c', 'y'), axis=0, tiled=True)]
    all_to_all x0 -> x4, waiting for transfers between devices: none -> 38.9 us  [a2a(): return lax.all_to_all(value, axes, 0, 0, tiled=True)]
    ppermute x0 -> x6, starting transfers between devices: none -> 33.1 us  [the longest x3 23.3 us: local(): moved = [lax.ppermute(blocks[k], 'zh', ring(k)) for k in (1, 3, 2)]]
    all_to_all x0 -> x4, starting transfers between devices: none -> 26 us  [a2a(): return lax.all_to_all(value, axes, 0, 0, tiled=True)]
    all_to_all x0 -> x1, blocking collectives: none -> 22.1 us  [a2a(): return lax.all_to_all(value, axes, 0, 0, tiled=True)]
    dot_general x3 -> x0, matrix products: 9.6 us -> none  [the longest x1 3.66 us: local(): lax.dot_general(attention, block_grads, (((0,), (0,)), ((), ())), preferr...]
  transfers between devices with their start and end apart: 3 -> 12, of which waited for: 3 -> 8; matrix products, arithmetic and copies ran while one was open for 1% -> 2% of each run, Pallas kernels for 0% -> 0%
where the time goes in v1:
time: 174 us; the launch traced here: 172 us
  waiting for transfers between devices  63.5 us (36%)
  starting transfers between devices  59.2 us (34%)
  blocking collectives  22.1 us (13%)
  between operations  14.2 us (8%)
  Pallas kernels  7.48 us (4%)
  local copies, waits for them, and re-layouts  4.42 us (3%)
    all_to_all x4, waiting for transfers between devices, a2a(): return lax.all_to_all(value, axes, 0, 0, tiled=True)  38.9 us
    all_to_all x4, starting transfers between devices, a2a(): return lax.all_to_all(value, axes, 0, 0, tiled=True)  26 us
    ppermute x3, starting transfers between devices, local(): moved = [lax.ppermute(blocks[k], 'zh', ring(k)) for k in (1, 3, 2)]  23.3 us
    all_to_all x1, blocking collectives, a2a(): return lax.all_to_all(value, axes, 0, 0, tiled=True)  22.1 us
    reduce_scatter x1, waiting for transfers between devices, local(): lax.psum_scatter(back, ('c', 'y'), scatter_dimension=0, tiled=True)  12.5 us
    ppermute x3, starting transfers between devices, local(): pieces = [grads] + [lax.ppermute(grads, 'x', ring(k)) for k in (1, 3, 2)]  9.81 us
    all_gather x1, waiting for transfers between devices, local(): att_all = lax.all_gather(attention, ('c', 'y'), axis=0, tiled=True)  7.09 us
    pallas_call x4, Pallas kernels, call(): pl.pallas_call(kernel, out_shape=out_shape, in_specs=specs, compiler_para...  6.11 us
  transfers between devices with their start and end apart: 12, of which 8 were waited for; matrix products, arithmetic and copies ran while one was open for 2% of the time, Pallas kernels for 0%

profile of v1, /device:TPU:6, one launch (start us, length us, event | category | flops | bytes accessed | tf_op | source)
XLA Modules:
  0.0 172.4 jit_solution(10607553302061211345)
XLA Ops:
  7.2 0.0 copy-start
  7.2 1.6 copy-done
  8.8 0.9 copy-done.2
  9.7 2.0 %shard_map.109 = (bf16[256,4096]{1,0:T(8,128)(2,1)}, bf16[256,512]{1,0:T(8,128)(2,1)S(1)}) custom-call(s32[1]{0:T(128)} %bitcast.yc_ref, bf16[256,256]{1,0:T(8,128)(2,1)S(1)} %copy-done.2, bf16[256,4096]{1,0:T(8,128)(2,1)S(1)} %copy-done), custom_call_target="tpu_custom_call" | custom-call | tf_op jit(solution)/shard_map/pallas_call | solution.py:21
  11.7 9.4 %all-to-all-start = ((bf16[4,64,4096]{2,1,0:T(8,128)(2,1)}), bf16[4,64,4096]{2,1,0:T(8,128)(2,1)S(1)}, u32[]{:S(2)}, u32[]{:S(2)}) async-start(bf16[4,64,4096]{2,1,0:T(8,128)(2,1)} %bitcast.1), calls=%async_computation | async-start | bytes 4194304 | tf_op jit(solution)/shard_map/all_to_all | solution.py:25
  21.2 0.0 all-gather.2.cloned.1.call-start
  21.2 0.7 all-gather.2.cloned.1.call-update
  21.9 18.9 %all-to-all-done = bf16[4,64,4096]{2,1,0:T(8,128)(2,1)S(1)} async-done(((bf16[4,64,4096]{2,1,0:T(8,128)(2,1)}), bf16[4,64,4096]{2,1,0:T(8,128)(2,1)S(1)}, u32[]{:S(2)}, u32[]{:S(2)}) %all-to-all-start) | async-done | bytes 2097184 | tf_op jit(solution)/shard_map/all_to_all | solution.py:25
  40.7 1.3 reduce_sum.30
  42.0 5.9 %all-to-all-start.1 = ((bf16[4,16,4096]{2,1,0:T(8,128)(2,1)}), bf16[4,16,4096]{2,1,0:T(8,128)(2,1)S(1)}, u32[]{:S(2)}, u32[]{:S(2)}) async-start(bf16[4,16,4096]{2,1,0:T(8,128)(2,1)} %bitcast.26), calls=%async_computation.1 | async-start | bytes 1048576 | tf_op jit(solution)/shard_map/all_to_all | solution.py:25
  47.9 7.1 %all-gather.2.cloned.1.call-done = bf16[2048,256]{1,0:T(8,128)(2,1)} async-done(((bf16[256,256]{1,0:T(8,128)(2,1)}), bf16[2048,256]{1,0:T(8,128)(2,1)}) %all-gather.2.cloned.1.call-update) | async-done | bytes 1048592 | tf_op jit(solution)/shard_map/all_gather | solution.py:118
  55.0 6.2 %all-to-all-done.1.parts_ref = bf16[4,16,4096]{2,1,0:T(8,128)(2,1)S(1)} async-done(((bf16[4,16,4096]{2,1,0:T(8,128)(2,1)}), bf16[4,16,4096]{2,1,0:T(8,128)(2,1)S(1)}, u32[]{:S(2)}, u32[]{:S(2)}) %all-to-all-start.1) | async-done | bytes 524320 | tf_op jit(solution)/shard_map/all_to_all | solution.py:25
  61.2 0.0 copy-done.3
  61.2 0.0 copy-done.4
  61.2 0.0 copy-done.5
  61.2 0.0 copy-done.6
  61.2 1.1 shard_map.110
  62.3 22.1 %all_to_all.33 = bf16[32,16,512]{2,1,0:T(8,128)(2,1)S(1)} all-to-all(bf16[32,16,512]{2,1,0:T(8,128)(2,1)S(1)} %get-tuple-element.30), channel_id=1, replica_groups=mesh['zh'=4,'y'=4,'c'=2,'zl'=4,'x'=4] {'c','y','zl'}, dimensions={0} | all-to-all | bytes 1048576 | tf_op jit(solution)/shard_map/all_to_all | solution.py:25
  84.4 4.0 %collective-permute-start = (bf16[512,512]{1,0:T(8,128)(2,1)S(1)}, bf16[512,512]{1,0:T(8,128)(2,1)S(1)}, u32[]{:S(2)}, u32[]{:S(2)}) collective-permute-start(bf16[512,512]{1,0:T(8,128)(2,1)S(1)} %bitcast.17), channel_id=1, source_target_pairs={{0,1},{1,2},{2,3},{3,0},{4,5},{5,6},{6,7},{7,4},{8,9},{9,10},{10,1... | collective-permute-start | bytes 1572872 | tf_op jit(solution)/shard_map/ppermute | solution.py:136
  88.4 1.9 %collective-permute-start.1 = (bf16[512,512]{1,0:T(8,128)(2,1)S(1)}, bf16[512,512]{1,0:T(8,128)(2,1)S(1)}, u32[]{:S(2)}, u32[]{:S(2)}) collective-permute-start(bf16[512,512]{1,0:T(8,128)(2,1)S(1)} %bitcast.18), channel_id=1, source_target_pairs={{0,3},{1,0},{2,1},{3,2},{4,7},{5,4},{6,5},{7,6},{8,11},{9,8},{10,9... | collective-permute-start | bytes 1572872 | tf_op jit(solution)/shard_map/ppermute | solution.py:136
  90.3 3.9 %collective-permute-start.2 = (bf16[512,512]{1,0:T(8,128)(2,1)S(1)}, bf16[512,512]{1,0:T(8,128)(2,1)S(1)}, u32[]{:S(2)}, u32[]{:S(2)}) collective-permute-start(bf16[512,512]{1,0:T(8,128)(2,1)S(1)} %bitcast.19), channel_id=1, source_target_pairs={{0,2},{1,3},{2,0},{3,1},{4,6},{5,7},{6,4},{7,5},{8,10},{9,11},{10,... | collective-permute-start | bytes 1572872 | tf_op jit(solution)/shard_map/ppermute | solution.py:136
  94.3 4.0 %all-to-all-start.3 = ((f32[32,1,512]{2,1,0:T(1,128)}), f32[32,1,512]{2,1,0:T(1,128)S(1)}, u32[]{:S(2)}, u32[]{:S(2)}) async-start(f32[32,1,512]{2,1,0:T(1,128)} %get-tuple-element.32), calls=%async_computation.3 | async-start | bytes 131072 | tf_op jit(solution)/shard_map/all_to_all | solution.py:25
  98.3 8.1 %all-to-all-done.3 = f32[32,1,512]{2,1,0:T(1,128)S(1)} async-done(((f32[32,1,512]{2,1,0:T(1,128)}), f32[32,1,512]{2,1,0:T(1,128)S(1)}, u32[]{:S(2)}, u32[]{:S(2)}) %all-to-all-start.3) | async-done | bytes 65568 | tf_op jit(solution)/shard_map/all_to_all | solution.py:25
  106.4 0.1 reduce_sum.31
  106.5 0.7 broadcast_in_dim.2
  107.2 6.7 %all-to-all-start.4 = ((f32[32,1,512]{2,1,0:T(1,128)}), f32[32,1,512]{2,1,0:T(1,128)S(1)}, u32[]{:S(2)}, u32[]{:S(2)}) async-start(f32[32,1,512]{2,1,0:T(1,128)} %broadcast_in_dim.2), calls=%async_computation.4 | async-start | bytes 131072 | tf_op jit(solution)/shard_map/all_to_all | solution.py:25
  113.8 0.0 reduce-scatter.2.cloned.1.call-start
  113.9 0.1 pad_add_fusion.at_ref
  113.9 5.7 %all-to-all-done.4 = f32[32,1,512]{2,1,0:T(1,128)S(1)} async-done(((f32[32,1,512]{2,1,0:T(1,128)}), f32[32,1,512]{2,1,0:T(1,128)S(1)}, u32[]{:S(2)}, u32[]{:S(2)}) %all-to-all-start.4) | async-done | bytes 65568 | tf_op jit(solution)/shard_map/all_to_all | solution.py:25
  119.7 0.0 collective-permute-done.refs_1_
  119.7 0.0 collective-permute-done.1.refs_2_
  119.7 0.0 collective-permute-done.2.refs_3_
  119.7 0.0 copy-done.1
  119.7 1.4 shard_map.111
  121.1 0.0 copy-start.7
  121.1 0.6 copy-done.7
  121.7 2.3 %shard_map.112 = bf16[8,4,4,16,256]{4,3,2,1,0:T(8,128)(2,1)} custom-call(s32[3]{0:T(128)S(1)} %pad_add_fusion.at_ref, bf16[256,512]{1,0:T(8,128)(2,1)S(1)} %get-tuple-element.36.weight_ref, bf16[512,512]{1,0:T(8,128)(2,1)S(1)} %bitcast.21, bf16[512,512]{1,0:T(8,128)(2,1)S(1)} %collective-permute-done.refs_1_, ...), custom_call_target="tpu_custom_call" | custom-call | tf_op jit(solution)/shard_map/pallas_call | solution.py:21
  124.0 0.0 copy-done.10
  124.0 0.0 reduce-scatter.2.cloned.1.call-update
  124.0 9.1 %collective-permute-start.3 = (bf16[320,128]{1,0:T(8,128)(2,1)}, bf16[320,128]{1,0:T(8,128)(2,1)S(1)}, u32[]{:S(2)}, u32[]{:S(2)}) collective-permute-start(bf16[320,128]{1,0:T(8,128)(2,1)} %copy-done.10), channel_id=1, source_target_pairs={{0,128},{128,256},{256,384},{384,0},{1,129},{129,257},{257,385},{3... | collective-permute-start | bytes 245768 | tf_op jit(solution)/shard_map/ppermute | solution.py:149
  133.1 3.4 %collective-permute-start.4 = (bf16[320,128]{1,0:T(8,128)(2,1)}, bf16[320,128]{1,0:T(8,128)(2,1)S(1)}, u32[]{:S(2)}, u32[]{:S(2)}) collective-permute-start(bf16[320,128]{1,0:T(8,128)(2,1)} %copy-done.9), channel_id=1, source_target_pairs={{0,384},{128,0},{256,128},{384,256},{1,385},{129,1},{257,129},{385... | collective-permute-start | bytes 245768 | tf_op jit(solution)/shard_map/ppermute | solution.py:149
  136.5 10.8 %collective-permute-start.5 = (bf16[320,128]{1,0:T(8,128)(2,1)S(1)}, bf16[320,128]{1,0:T(8,128)(2,1)S(1)}, u32[]{:S(2)}, u32[]{:S(2)}) collective-permute-start(bf16[320,128]{1,0:T(8,128)(2,1)S(1)} %copy-done.8), channel_id=1, source_target_pairs={{0,256},{128,384},{256,0},{384,128},{1,257},{129,385},{257,1},{385... | collective-permute-start | bytes 245768 | tf_op jit(solution)/shard_map/ppermute | solution.py:149
  147.4 0.0 collective-permute-done.3.refs_1_
  147.4 0.8 collective-permute-done.4.refs_2_
  148.2 3.5 %collective-permute-done.5.refs_3_ = bf16[320,128]{1,0:T(8,128)(2,1)S(1)} collective-permute-done((bf16[320,128]{1,0:T(8,128)(2,1)S(1)}, bf16[320,128]{1,0:T(8,128)(2,1)S(1)}, u32[]{:S(2)}, u32[]{:S(2)}) %collective-permute-start.5) | collective-permute-done | bytes 81952 | tf_op jit(solution)/shard_map/ppermute | solution.py:149
  151.7 0.7 shard_map.113
  152.4 0.6 copy.20
  153.0 12.5 %reduce-scatter.2.cloned.1.call-done = bf16[1,256,256]{2,1,0:T(8,128)(2,1)} async-done(((bf16[8,256,256]{2,1,0:T(8,128)(2,1)}), bf16[1,256,256]{2,1,0:T(8,128)(2,1)}) %reduce-scatter.2.cloned.1.call-update) | async-done | bytes 131088 | tf_op jit(solution)/shard_map/reduce_scatter | solution.py:158
  (12 shorter events, 0.0 us)
Async XLA Ops:
  7.2 1.6 copy-start
  8.8 0.9 copy-start.2
  11.7 29.0 %all-to-all-start = ((bf16[4,64,4096]{2,1,0:T(8,128)(2,1)}), bf16[4,64,4096]{2,1,0:T(8,128)(2,1)S(1)}, u32[]{:S(2)}, u32[]{:S(2)}) async-start(bf16[4,64,4096]{2,1,0:T(8,128)(2,1)} %bitcast.1), calls=%async_computation | async-start | bytes 4194304 | tf_op jit(solution)/shard_map/all_to_all | solution.py:25
  21.1 40.1 %copy-start.3 = (bf16[16,4096]{1,0:T(8,128)(2,1)S(1)}, bf16[16,4096]{1,0:T(8,128)(2,1)}, u32[]{:S(2)}) copy-start(bf16[16,4096]{1,0:T(8,128)(2,1)} %residual_ref.1) | copy-start | bytes 393220
  21.1 40.1 %copy-start.4 = (bf16[16,4096]{1,0:T(8,128)(2,1)S(1)}, bf16[16,4096]{1,0:T(8,128)(2,1)}, u32[]{:S(2)}) copy-start(bf16[16,4096]{1,0:T(8,128)(2,1)} %upstream_ref.1) | copy-start | bytes 393220
  21.1 40.1 %copy-start.5 = (bf16[16,4096]{1,0:T(8,128)(2,1)S(1)}, bf16[16,4096]{1,0:T(8,128)(2,1)}, u32[]{:S(2)}) copy-start(bf16[16,4096]{1,0:T(8,128)(2,1)} %resid_grad_ref.1) | copy-start | bytes 393220
  21.1 40.1 %copy-start.6 = (f32[4096]{0:T(1024)S(1)}, f32[4096]{0:T(1024)}, u32[]{:S(2)}) copy-start(f32[4096]{0:T(1024)} %param.9) | copy-start | bytes 49156
  21.2 33.9 %all-gather.2.cloned.1.call-start = ((), (), s32[]{:S(2)}) async-start(), calls=%async_computation.6 | async-start | bytes 1179648 | tf_op jit(solution)/shard_map/all_gather | solution.py:118
  42.0 19.2 %all-to-all-start.1 = ((bf16[4,16,4096]{2,1,0:T(8,128)(2,1)}), bf16[4,16,4096]{2,1,0:T(8,128)(2,1)S(1)}, u32[]{:S(2)}, u32[]{:S(2)}) async-start(bf16[4,16,4096]{2,1,0:T(8,128)(2,1)} %bitcast.26), calls=%async_computation.1 | async-start | bytes 1048576 | tf_op jit(solution)/shard_map/all_to_all | solution.py:25
  55.0 64.7 %copy-start.1 = (bf16[2048,256]{1,0:T(8,128)(2,1)S(1)}, bf16[2048,256]{1,0:T(8,128)(2,1)}, u32[]{:S(2)}) copy-start(bf16[2048,256]{1,0:T(8,128)(2,1)} %all-gather.2.cloned.1.call-done) | copy-start | bytes 3145732
  84.4 35.2 %collective-permute-start = (bf16[512,512]{1,0:T(8,128)(2,1)S(1)}, bf16[512,512]{1,0:T(8,128)(2,1)S(1)}, u32[]{:S(2)}, u32[]{:S(2)}) collective-permute-start(bf16[512,512]{1,0:T(8,128)(2,1)S(1)} %bitcast.17), channel_id=1, source_target_pairs={{0,1},{1,2},{2,3},{3,0},{4,5},{5,6},{6,7},{7,4},{8,9},{9,10},{10,1... | collective-permute-start | bytes 1572872 | tf_op jit(solution)/shard_map/ppermute | solution.py:136
  88.4 31.3 %collective-permute-start.1 = (bf16[512,512]{1,0:T(8,128)(2,1)S(1)}, bf16[512,512]{1,0:T(8,128)(2,1)S(1)}, u32[]{:S(2)}, u32[]{:S(2)}) collective-permute-start(bf16[512,512]{1,0:T(8,128)(2,1)S(1)} %bitcast.18), channel_id=1, source_target_pairs={{0,3},{1,0},{2,1},{3,2},{4,7},{5,4},{6,5},{7,6},{8,11},{9,8},{10,9... | collective-permute-start | bytes 1572872 | tf_op jit(solution)/shard_map/ppermute | solution.py:136
  90.3 29.4 %collective-permute-start.2 = (bf16[512,512]{1,0:T(8,128)(2,1)S(1)}, bf16[512,512]{1,0:T(8,128)(2,1)S(1)}, u32[]{:S(2)}, u32[]{:S(2)}) collective-permute-start(bf16[512,512]{1,0:T(8,128)(2,1)S(1)} %bitcast.19), channel_id=1, source_target_pairs={{0,2},{1,3},{2,0},{3,1},{4,6},{5,7},{6,4},{7,5},{8,10},{9,11},{10,... | collective-permute-start | bytes 1572872 | tf_op jit(solution)/shard_map/ppermute | solution.py:136
  94.3 12.1 %all-to-all-start.3 = ((f32[32,1,512]{2,1,0:T(1,128)}), f32[32,1,512]{2,1,0:T(1,128)S(1)}, u32[]{:S(2)}, u32[]{:S(2)}) async-start(f32[32,1,512]{2,1,0:T(1,128)} %get-tuple-element.32), calls=%async_computation.3 | async-start | bytes 131072 | tf_op jit(solution)/shard_map/all_to_all | solution.py:25
  107.2 12.5 %all-to-all-start.4 = ((f32[32,1,512]{2,1,0:T(1,128)}), f32[32,1,512]{2,1,0:T(1,128)S(1)}, u32[]{:S(2)}, u32[]{:S(2)}) async-start(f32[32,1,512]{2,1,0:T(1,128)} %broadcast_in_dim.2), calls=%async_computation.4 | async-start | bytes 131072 | tf_op jit(solution)/shard_map/all_to_all | solution.py:25
  113.8 51.7 %reduce-scatter.2.cloned.1.call-start = ((), (), s32[]{:S(2)}) async-start(), calls=%async_computation.7 | async-start | bytes 1179648 | tf_op jit(solution)/shard_map/reduce_scatter | solution.py:158
  121.1 0.6 copy-start.7
  121.7 2.3 %copy-start.9 = (bf16[320,128]{1,0:T(8,128)(2,1)}, bf16[320,128]{1,0:T(8,128)(2,1)S(1)}, u32[]{:S(2)}) copy-start(bf16[320,128]{1,0:T(8,128)(2,1)S(1)} %get-tuple-element.38) | copy-start | bytes 245764
  121.7 2.3 %copy-start.10 = (bf16[320,128]{1,0:T(8,128)(2,1)}, bf16[320,128]{1,0:T(8,128)(2,1)S(1)}, u32[]{:S(2)}) copy-start(bf16[320,128]{1,0:T(8,128)(2,1)S(1)} %get-tuple-element.37) | copy-start | bytes 245764
  121.7 14.8 %copy-start.8 = (bf16[320,128]{1,0:T(8,128)(2,1)S(1)}, bf16[320,128]{1,0:T(8,128)(2,1)}, u32[]{:S(2)}) copy-start(bf16[320,128]{1,0:T(8,128)(2,1)} %copy-done.7) | copy-start | bytes 245764
  124.0 23.3 %collective-permute-start.3 = (bf16[320,128]{1,0:T(8,128)(2,1)}, bf16[320,128]{1,0:T(8,128)(2,1)S(1)}, u32[]{:S(2)}, u32[]{:S(2)}) collective-permute-start(bf16[320,128]{1,0:T(8,128)(2,1)} %copy-done.10), channel_id=1, source_target_pairs={{0,128},{128,256},{256,384},{384,0},{1,129},{129,257},{257,385},{3... | collective-permute-start | bytes 245768 | tf_op jit(solution)/shard_map/ppermute | solution.py:149
  133.1 15.0 %collective-permute-start.4 = (bf16[320,128]{1,0:T(8,128)(2,1)}, bf16[320,128]{1,0:T(8,128)(2,1)S(1)}, u32[]{:S(2)}, u32[]{:S(2)}) collective-permute-start(bf16[320,128]{1,0:T(8,128)(2,1)} %copy-done.9), channel_id=1, source_target_pairs={{0,384},{128,0},{256,128},{384,256},{1,385},{129,1},{257,129},{385... | collective-permute-start | bytes 245768 | tf_op jit(solution)/shard_map/ppermute | solution.py:149
  136.5 15.1 %collective-permute-start.5 = (bf16[320,128]{1,0:T(8,128)(2,1)S(1)}, bf16[320,128]{1,0:T(8,128)(2,1)S(1)}, u32[]{:S(2)}, u32[]{:S(2)}) collective-permute-start(bf16[320,128]{1,0:T(8,128)(2,1)S(1)} %copy-done.8), channel_id=1, source_target_pairs={{0,256},{128,384},{256,0},{384,128},{1,257},{129,385},{257,1},{385... | collective-permute-start | bytes 245768 | tf_op jit(solution)/shard_map/ppermute | solution.py:149
Sparse Core Ops, SparseCore 0:
  24.1 30.8 all-gather.1
  124.1 41.3 reduce-scatter.1

commit v2 on v1

v2 whole, which is shorter than its diff:
```python
import jax
import jax.numpy as jnp
from jax import lax
from jax.experimental import pallas as pl
from jax.experimental.pallas import tpu as pltpu
from jax.sharding import Mesh, PartitionSpec as P

BF16, F32 = jnp.bfloat16, jnp.float32
AXES = ("zh", "y", "c", "zl", "x")
PARAMS = pltpu.CompilerParams(vmem_limit_bytes=48 * 2**20)
SCALAR = pl.BlockSpec(memory_space=pltpu.SMEM)
WHOLE = pl.BlockSpec(memory_space=pltpu.VMEM)


def shape(dims, dtype=BF16):
    return jax.ShapeDtypeStruct(dims, dtype)


def call(kernel, out_shape, *args):
    specs = [SCALAR if a.dtype == jnp.int32 else WHOLE for a in args]
    return pl.pallas_call(kernel, out_shape=out_shape, in_specs=specs, compiler_params=PARAMS)(*args)


def a2a(value, axes):
    return lax.all_to_all(value, axes, 0, 0, tiled=True)


def ring(step):
    return [(i, (i + step) % 4) for i in range(4)]


def regroup_kernel(att_ref, out_ref):
    for x in range(4):
        for z in range(4):
            rows = att_ref[z * 64 + x * 16 : z * 64 + x * 16 + 16]
            for y in range(4):
                out_ref[y * 4 + x, z * 16 : z * 16 + 16] = rows


def columns_kernel(yc_ref, weight_ref, out_ref, sems):
    copies = [
        pltpu.make_async_copy(
            weight_ref.at[:, pl.ds(pl.multiple_of(yc_ref[0] * 128 + h * 1024, 128), 128)],
            out_ref.at[:, h * 128 : h * 128 + 128],
            sems.at[h],
        )
        for h in range(4)
    ]
    for copy in copies:
        copy.start()
    for copy in copies:
        copy.wait()


def columns(yc, weight):
    return pl.pallas_call(
        columns_kernel,
        out_shape=shape((256, 512)),
        in_specs=[SCALAR, pl.BlockSpec(memory_space=pl.ANY)],
        scratch_shapes=[pltpu.SemaphoreType.DMA((4,))],
    )(yc, weight)


def forward_kernel(c_ref, own_ref, other_ref, *refs):
    c, x = c_ref[0], c_ref[1]
    for att_ref, core in ((own_ref, c), (other_ref, 1 - c)):
        total = jnp.zeros((256, 512), F32)
        for j in range(4):
            att = att_ref[:, lax.rem(x + j, 4)].reshape(256, 256)
            total += jnp.dot(att, refs[j][...], preferred_element_type=F32)
        refs[4][pl.ds(core * 16, 16)] = total.astype(BF16).reshape(16, 16, 512)


def norm_kernel(
    parts_ref, residual_ref, gain_ref, upstream_ref, resid_grad_ref,
    normed_ref, stream_ref, grad_ref, cols_ref, projected_ref,
):
    for c in range(2):
        for y in range(4):
            at = (c * 4 + y) * 4
            total = parts_ref[at].astype(F32)
            for k in range(1, 4):
                total += parts_ref[at + k].astype(F32)
            for h in range(4):
                start = (h * 8 + y * 2 + c) * 128
                projected_ref[:, start : start + 128] = total[:, h * 128 : h * 128 + 128]
    projected = projected_ref[...]
    stream_out = (residual_ref[...].astype(F32) + projected).astype(BF16)
    stream_ref[...] = stream_out
    values = stream_out.astype(F32)
    inv_rms = lax.rsqrt(jnp.mean(values * values, axis=-1, keepdims=True) + 1e-05)
    unit_rows = values * inv_rms
    gain = gain_ref[...]
    normed_ref[...] = (unit_rows * gain).astype(BF16)
    upstream = upstream_ref[...].astype(F32)
    gain_grad = jnp.sum(upstream * unit_rows, axis=0, keepdims=True)
    scaled = upstream * gain
    inner = jnp.mean(scaled * unit_rows, axis=-1, keepdims=True)
    grad = (resid_grad_ref[...].astype(F32) + inv_rms * (scaled - unit_rows * inner)).astype(BF16)
    grad_ref[...] = grad
    for k in range(32):
        rows = jnp.broadcast_to(gain_grad[:, k * 128 : k * 128 + 128], (32, 128))
        cols_ref[:, 64 + k : 65 + k] = rows.astype(BF16)[:, None]
    for c in range(2):
        for y in range(4):
            for h in range(4):
                start = (h * 8 + y * 2 + c) * 128
                for z in range(4):
                    to = (c * 4 + y) * 4 + z
                    cols_ref[to, h * 16 : h * 16 + 16] = grad[:, start : start + 128]


def unpack_kernel(parts_ref, grads_ref, gain_ref):
    gain_ref[...] = jnp.sum(parts_ref[:, 64:].astype(F32), axis=0)
    for h in range(4):
        grads_ref[:, h * 128 : h * 128 + 128] = parts_ref[:, h * 16 : h * 16 + 16].reshape(512, 128)


def weight_kernel(at_ref, own_ref, other_ref, grads_ref, gain_ref, out_ref):
    c = at_ref[0]
    gain = gain_ref[...]
    upper = gain.astype(BF16)
    lower = (gain - upper.astype(F32)).astype(BF16)
    for x in range(4):
        total = jnp.zeros((256, 512), F32)
        for att_ref, core in ((own_ref, c), (other_ref, 1 - c)):
            total += lax.dot_general(
                att_ref[:, x].reshape(256, 256),
                grads_ref[pl.ds(pl.multiple_of(core * 256, 256), 256)],
                (((0,), (0,)), ((), ())),
                preferred_element_type=F32,
            )
        total = total.astype(BF16)
        for h in range(4):
            out_ref[x, h * 256 : h * 256 + 256] = total[:, h * 128 : h * 128 + 128]
        out_ref[x, 1024:1056] = upper
        out_ref[x, 1056:] = lower


def weight_x_kernel(parts_ref, out_ref):
    total = parts_ref[0].astype(F32)
    for k in range(1, 4):
        total += parts_ref[k].astype(F32)
    for h in range(4):
        out_ref[h, :256] = total[h * 256 : h * 256 + 256].astype(BF16)
        out_ref[h, 256:] = (total[1024:1056] + total[1056:]).astype(BF16)


def weight_zh_kernel(parts_ref, weight_ref, gain_ref):
    total = parts_ref[0].astype(F32)
    for k in range(1, 4):
        total += parts_ref[k].astype(F32)
    weight_ref[...] = total[:256]
    gain_ref[...] = total[256:]


def back_kernel(at_ref, grads_ref, *refs):
    for out_ref, core in ((refs[4], 1 - at_ref[0]), (refs[5], at_ref[0])):
        rows = grads_ref[pl.ds(pl.multiple_of(core * 256, 256), 256)]
        for j in range(4):
            back = lax.dot_general(
                rows, refs[j][...], (((1,), (1,)), ((), ())), preferred_element_type=F32
            )
            back = back.reshape(4, 64, 256).astype(out_ref.dtype)
            for y in range(4):
                out_ref[lax.rem(y + 4 - at_ref[2], 4), j] = back[y]


def add_core_kernel(keep_ref, other_ref, *refs):
    for j in range(4):
        refs[j][...] = (keep_ref[j] + other_ref[j].astype(F32)).astype(BF16)


def add_y_kernel(*refs):
    total = refs[0][...].astype(F32)
    for ref in refs[1:4]:
        total += ref[...].astype(F32)
    for j in range(4):
        refs[4 + j][...] = total[j].astype(BF16)


def join_kernel(at_ref, *refs):
    for ref, step in zip(refs[:4], (0, 3, 1, 2)):
        refs[4][:, lax.rem(at_ref[1] + step, 4)] = ref[...].reshape(4, 16, 256)


def local(attention, residual, out_weight, norm_gain, grad_normed, grad_resid):
    x, y, c = (lax.axis_index(n).astype(jnp.int32) for n in ("x", "y", "c"))
    at = jnp.stack([c, x, y])
    swap = [(0, 1), (1, 0)]

    weight = columns((y * 2 + c).reshape(1), out_weight)
    weights = [weight] + [lax.ppermute(weight, "x", ring(4 - j)) for j in (1, 2, 3)]

    own = call(regroup_kernel, shape((16, 64, 256)), attention)
    own = a2a(own, ("y", "x")).reshape(4, 4, 64, 256)
    own, *weights = lax.optimization_barrier((own, *weights))
    other = lax.ppermute(own, "c", swap)

    parts = call(forward_kernel, shape((32, 16, 512)), at, own, other, *weights)
    parts = a2a(parts, ("c", "y", "zl"))

    normed, stream_out, stream_grad, cols = pl.pallas_call(
        norm_kernel,
        out_shape=(shape((16, 4096)),) * 3 + (shape((32, 96, 128)),),
        in_specs=[WHOLE] * 5,
        scratch_shapes=[pltpu.VMEM((16, 4096), F32)],
        compiler_params=PARAMS,
    )(parts, residual, norm_gain.reshape(1, 4096), grad_normed, grad_resid)

    grads, gain = call(
        unpack_kernel, (shape((512, 512)), shape((32, 128), F32)), a2a(cols, ("c", "y", "zl"))
    )

    blocks = call(weight_kernel, shape((4, 1088, 128)), at, own, other, grads, gain)
    blocks, weights[0] = lax.optimization_barrier((blocks, weights[0]))
    by_zh = call(weight_x_kernel, shape((4, 288, 128)), a2a(blocks, "x"))

    send, keep = call(
        back_kernel,
        (shape((4, 4, 64, 256)), shape((4, 4, 64, 256), F32)),
        at,
        grads,
        *weights,
    )
    back = call(add_core_kernel, (shape((4, 64, 256)),) * 4, keep, lax.ppermute(send, "c", swap))
    moved = [lax.ppermute(back[k], "y", ring(k)) for k in (1, 3, 2)]
    by_zh, moved[0] = lax.optimization_barrier((by_zh, moved[0]))
    parts = a2a(by_zh, "zh")
    back = call(add_y_kernel, (shape((64, 256)),) * 4, back[0], *moved)
    moved = [lax.ppermute(back[k], "x", ring(k)) for k in (1, 3, 2)]
    parts, moved[2] = lax.optimization_barrier((parts, moved[2]))
    weight_grad, gain = call(
        weight_zh_kernel, (shape((256, 128), F32), shape((32, 128), F32)), parts
    )
    attn_grad = call(join_kernel, shape((4, 4, 16, 256)), at, back[0], *moved).reshape(256, 256)
    return (normed, stream_out, stream_grad, attn_grad, weight_grad, gain.reshape(4096))


def solution(mesh):
    fine = Mesh(mesh.devices.reshape(4, 4, 2, 4, 4), AXES)
    dp, tensor = ("zh", "y", "c"), ("zl", "x")
    rows = P(dp + tensor, None)
    return jax.shard_map(
        local,
        mesh=fine,
        in_specs=(P(dp, tensor), rows, P(tensor, None), P(), rows, rows),
        out_specs=(rows, rows, rows, P(dp, tensor), P(tensor, dp), P()),
        check_vma=False,
    )
```

time: 174 us -> 150 us (0.86)
  waiting for transfers between devices: 63.5 us -> 25.9 us
  blocking collectives: 22.1 us -> 50 us
  between operations: 14.2 us -> 0.83 us
  Pallas kernels: 7.48 us -> 11.6 us
  local copies, waits for them, and re-layouts: 4.42 us -> 1.87 us
    all_to_all x4 -> x3, waiting for transfers between devices: 38.9 us -> 4.77 us  [a2a(): return lax.all_to_all(value, axes, 0, 0, tiled=True)]
    all_to_all x1 -> x2, blocking collectives: 22.1 us -> 50 us  [a2a(): return lax.all_to_all(value, axes, 0, 0, tiled=True)]
    ppermute x6 -> x11, waiting for transfers between devices: 4.32 us -> 21.2 us  [the longest x3 9.05 us: local(): lax.ppermute(weight, 'x', ring(4 - j))]
    reduce_scatter x1 -> x0, waiting for transfers between devices: 12.5 us -> none  [local(): lax.psum_scatter(back, ('c', 'y'), scatter_dimension=0, tiled=True)]
    all_gather x1 -> x0, waiting for transfers between devices: 7.09 us -> none  [local(): att_all = lax.all_gather(attention, ('c', 'y'), axis=0, tiled=True)]
    pallas_call x4 -> x10, Pallas kernels: 6.11 us -> 8.66 us  [call(): pl.pallas_call(kernel, out_shape=out_shape, in_specs=specs, compiler_para...]
    ppermute x6 -> x11, starting transfers between devices: 33.1 us -> 32.3 us  [the longest x3 10.2 us: local(): moved = [lax.ppermute(back[k], 'y', ring(k)) for k in (1, 3, 2)]]
    all_to_all x4 -> x3, starting transfers between devices: 26 us -> 26.6 us  [a2a(): return lax.all_to_all(value, axes, 0, 0, tiled=True)]
  transfers between devices with their start and end apart: 12 -> 14, of which waited for: 8 -> 9; matrix products, arithmetic and copies ran while one was open for 2% -> 0% of each run, Pallas kernels for 0% -> 3%
where the time goes in v2:
time: 150 us; the launch traced here: 149 us
  starting transfers between devices  58.9 us (39%)
  blocking collectives  50 us (33%)
  waiting for transfers between devices  25.9 us (17%)
  Pallas kernels  11.6 us (8%)
  local copies, waits for them, and re-layouts  1.87 us (1%)
    all_to_all x2, blocking collectives, a2a(): return lax.all_to_all(value, axes, 0, 0, tiled=True)  50 us
    all_to_all x3, starting transfers between devices, a2a(): return lax.all_to_all(value, axes, 0, 0, tiled=True)  26.6 us
    ppermute x3, starting transfers between devices, local(): moved = [lax.ppermute(back[k], 'y', ring(k)) for k in (1, 3, 2)]  10.2 us
    ppermute x3, starting transfers between devices, local(): moved = [lax.ppermute(back[k], 'x', ring(k)) for k in (1, 3, 2)]  9.7 us
    ppermute x3, waiting for transfers between devices, local(): lax.ppermute(weight, 'x', ring(4 - j))  9.05 us
    pallas_call x10, Pallas kernels, call(): pl.pallas_call(kernel, out_shape=out_shape, in_specs=specs, compiler_para...  8.66 us
    ppermute x3, starting transfers between devices, local(): lax.ppermute(weight, 'x', ring(4 - j))  8.65 us
    ppermute x3, waiting for transfers between devices, local(): moved = [lax.ppermute(back[k], 'y', ring(k)) for k in (1, 3, 2)]  5.39 us
  transfers between devices with their start and end apart: 14, of which 9 were waited for; matrix products, arithmetic and copies ran while one was open for 0% of the time, Pallas kernels for 3%

profile of v2, /device:TPU:6, one launch (start us, length us, event | category | flops | bytes accessed | tf_op | source)
XLA Modules:
  0.0 149.2 jit_solution(1167685753253566944)
XLA Ops:
  0.6 0.9 copy-done.2
  1.5 0.8 shard_map.109
  2.4 9.2 %all-to-all-start = ((bf16[16,64,256]{2,1,0:T(8,128)(2,1)}), bf16[16,64,256]{2,1,0:T(8,128)(2,1)S(1)}, u32[]{:S(2)}, u32[]{:S(2)}) async-start(bf16[16,64,256]{2,1,0:T(8,128)(2,1)} %shard_map.109), calls=%async_computation | async-start | bytes 1048576 | tf_op jit(solution)/shard_map/all_to_all | solution.py:25
  11.6 1.7 %shard_map.110.refs_0_ = bf16[256,512]{1,0:T(8,128)(2,1)} custom-call(s32[1]{0:T(128)} %bitcast.4.yc_ref, bf16[256,4096]{1,0:T(8,128)(2,1)} %weight_ref.1), custom_call_target="tpu_custom_call" | custom-call | tf_op jit(solution)/shard_map/pallas_call | solution.py:56
  13.3 2.1 %collective-permute-start.2 = (bf16[256,512]{1,0:T(8,128)(2,1)}, bf16[256,512]{1,0:T(8,128)(2,1)S(1)}, u32[]{:S(2)}, u32[]{:S(2)}) collective-permute-start(bf16[256,512]{1,0:T(8,128)(2,1)} %shard_map.110.refs_0_), channel_id=1, source_target_pairs={{0,1},{1,2},{2,3},{3,0},{4,5},{5,6},{6,7},{7,4},{8,9},{9,10},{10,1... | collective-permute-start | bytes 786440 | tf_op jit(solution)/shard_map/ppermute | solution.py:193
  15.4 4.6 %collective-permute-start.1 = (bf16[256,512]{1,0:T(8,128)(2,1)}, bf16[256,512]{1,0:T(8,128)(2,1)S(1)}, u32[]{:S(2)}, u32[]{:S(2)}) collective-permute-start(bf16[256,512]{1,0:T(8,128)(2,1)} %shard_map.110.refs_0_), channel_id=1, source_target_pairs={{0,2},{1,3},{2,0},{3,1},{4,6},{5,7},{6,4},{7,5},{8,10},{9,11},{10,... | collective-permute-start | bytes 786440 | tf_op jit(solution)/shard_map/ppermute | solution.py:193
  20.0 1.9 %collective-permute-start = (bf16[256,512]{1,0:T(8,128)(2,1)}, bf16[256,512]{1,0:T(8,128)(2,1)S(1)}, u32[]{:S(2)}, u32[]{:S(2)}) collective-permute-start(bf16[256,512]{1,0:T(8,128)(2,1)} %shard_map.110.refs_0_), channel_id=1, source_target_pairs={{0,3},{1,0},{2,1},{3,2},{4,7},{5,4},{6,5},{7,6},{8,11},{9,8},{10,9... | collective-permute-start | bytes 786440 | tf_op jit(solution)/shard_map/ppermute | solution.py:193
  22.0 2.7 %collective-permute-done.2.refs_3_ = bf16[256,512]{1,0:T(8,128)(2,1)S(1)} collective-permute-done((bf16[256,512]{1,0:T(8,128)(2,1)}, bf16[256,512]{1,0:T(8,128)(2,1)S(1)}, u32[]{:S(2)}, u32[]{:S(2)}) %collective-permute-start.2) | collective-permute-done | bytes 262176 | tf_op jit(solution)/shard_map/ppermute | solution.py:193
  24.6 3.3 %collective-permute-done.1.refs_2_ = bf16[256,512]{1,0:T(8,128)(2,1)S(1)} collective-permute-done((bf16[256,512]{1,0:T(8,128)(2,1)}, bf16[256,512]{1,0:T(8,128)(2,1)S(1)}, u32[]{:S(2)}, u32[]{:S(2)}) %collective-permute-start.1) | collective-permute-done | bytes 262176 | tf_op jit(solution)/shard_map/ppermute | solution.py:193
  27.9 3.1 %collective-permute-done.refs_1_ = bf16[256,512]{1,0:T(8,128)(2,1)S(1)} collective-permute-done((bf16[256,512]{1,0:T(8,128)(2,1)}, bf16[256,512]{1,0:T(8,128)(2,1)S(1)}, u32[]{:S(2)}, u32[]{:S(2)}) %collective-permute-start) | collective-permute-done | bytes 262176 | tf_op jit(solution)/shard_map/ppermute | solution.py:193
  31.0 0.0 all-to-all-done
  31.0 1.9 %collective-permute-start.3 = (bf16[4,4,64,256]{3,2,1,0:T(8,128)(2,1)S(1)}, bf16[4,4,64,256]{3,2,1,0:T(8,128)(2,1)S(1)}, u32[]{:S(2)}, u32[]{:S(2)}) collective-permute-start(bf16[4,4,64,256]{3,2,1,0:T(8,128)(2,1)S(1)} %bitcast.8), channel_id=1, source_target_pairs={{0,16},{16,0},{1,17},{17,1},{2,18},{18,2},{3,19},{19,3},{4,20},{20... | collective-permute-start | bytes 1572872 | tf_op jit(solution)/shard_map/ppermute | solution.py:198
  32.9 0.1 pad_add_fusion.c_ref.at_ref
  33.0 1.8 %collective-permute-done.3.other_ref = bf16[4,4,64,256]{3,2,1,0:T(8,128)(2,1)S(1)} collective-permute-done((bf16[4,4,64,256]{3,2,1,0:T(8,128)(2,1)S(1)}, bf16[4,4,64,256]{3,2,1,0:T(8,128)(2,1)S(1)}, u32[]{:S(2)}, u32[]{:S(2)}) %collective-permute-start.3) | collective-permute-done | bytes 524320 | tf_op jit(solution)/shard_map/ppermute | solution.py:198
  34.8 0.9 copy-done
  35.8 1.2 shard_map.111
  37.0 0.0 copy-start.3
  37.0 0.0 copy-start.4
  37.0 0.0 copy-start.5
  37.1 24.6 %all_to_all.25.parts_ref = bf16[32,16,512]{2,1,0:T(8,128)(2,1)S(1)} all-to-all(bf16[32,16,512]{2,1,0:T(8,128)(2,1)S(1)} %shard_map.111), channel_id=1, replica_groups=mesh['zh'=4,'y'=4,'c'=2,'zl'=4,'x'=4] {'c','y','zl'}, dimensions={0} | all-to-all | bytes 1048576 | tf_op jit(solution)/shard_map/all_to_all | solution.py:25
  61.6 1.3 shard_map.112
  62.9 25.4 %all_to_all.26.parts_ref = bf16[32,96,128]{2,1,0:T(8,128)(2,1)S(1)} all-to-all(bf16[32,96,128]{2,1,0:T(8,128)(2,1)S(1)} %get-tuple-element.43), channel_id=1, replica_groups=mesh['zh'=4,'y'=4,'c'=2,'zl'=4,'x'=4] {'c','y','zl'}, dimensions={0} | all-to-all | bytes 1572864 | tf_op jit(solution)/shard_map/all_to_all | solution.py:25
  88.3 0.1 shard_map.113
  88.4 2.3 %shard_map.114 = bf16[4,1088,128]{2,1,0:T(8,128)(2,1)} custom-call(s32[3]{0:T(128)S(1)} %pad_add_fusion.c_ref.at_ref, bf16[4,4,64,256]{3,2,1,0:T(8,128)(2,1)S(1)} %bitcast.10, bf16[4,4,64,256]{3,2,1,0:T(8,128)(2,1)S(1)} %collective-permute-done.3.other_ref, bf16[512,512]{1,0:T(8,128)(2,1)S(1)} %get-tuple-element.44.grads_ref, ...), custom_call_target="tpu_custom_call" | custom-call | tf_op jit(solution)/shard_map/pallas_call | solution.py:21
  90.7 5.0 %all-to-all-start.3 = ((bf16[4,1088,128]{2,1,0:T(8,128)(2,1)}), bf16[4,1088,128]{2,1,0:T(8,128)(2,1)S(1)}, u32[]{:S(2)}, u32[]{:S(2)}) async-start(bf16[4,1088,128]{2,1,0:T(8,128)(2,1)} %shard_map.114), calls=%async_computation.3 | async-start | bytes 2228224 | tf_op jit(solution)/shard_map/all_to_all | solution.py:25
  95.7 1.3 shard_map.115
  97.0 1.9 %collective-permute-start.4 = (bf16[4,4,64,256]{3,2,1,0:T(8,128)(2,1)S(1)}, bf16[4,4,64,256]{3,2,1,0:T(8,128)(2,1)S(1)}, u32[]{:S(2)}, u32[]{:S(2)}) collective-permute-start(bf16[4,4,64,256]{3,2,1,0:T(8,128)(2,1)S(1)} %get-tuple-element.48), channel_id=1, source_target_pairs={{0,16},{16,0},{1,17},{17,1},{2,18},{18,2},{3,19},{19,3},{4,20},{20... | collective-permute-start | bytes 1572872 | tf_op jit(solution)/shard_map/ppermute | solution.py:226
  98.9 1.9 %collective-permute-done.4.other_ref = bf16[4,4,64,256]{3,2,1,0:T(8,128)(2,1)S(1)} collective-permute-done((bf16[4,4,64,256]{3,2,1,0:T(8,128)(2,1)S(1)}, bf16[4,4,64,256]{3,2,1,0:T(8,128)(2,1)S(1)}, u32[]{:S(2)}, u32[]{:S(2)}) %collective-permute-start.4) | collective-permute-done | bytes 524320 | tf_op jit(solution)/shard_map/ppermute | solution.py:226
  100.8 0.1 shard_map.116
  100.9 3.0 %collective-permute-start.5 = (bf16[4,64,256]{2,1,0:T(8,128)(2,1)S(1)}, bf16[4,64,256]{2,1,0:T(8,128)(2,1)S(1)}, u32[]{:S(2)}, u32[]{:S(2)}) collective-permute-start(bf16[4,64,256]{2,1,0:T(8,128)(2,1)S(1)} %get-tuple-element.51), channel_id=1, source_target_pairs={{0,32},{32,64},{64,96},{96,0},{1,33},{33,65},{65,97},{97,1},{2,34}... | collective-permute-start | bytes 393224 | tf_op jit(solution)/shard_map/ppermute | solution.py:227
  103.9 4.8 %all-to-all-done.3.parts_ref = bf16[4,1088,128]{2,1,0:T(8,128)(2,1)S(1)} async-done(((bf16[4,1088,128]{2,1,0:T(8,128)(2,1)}), bf16[4,1088,128]{2,1,0:T(8,128)(2,1)S(1)}, u32[]{:S(2)}, u32[]{:S(2)}) %all-to-all-start.3) | async-done | bytes 1114144 | tf_op jit(solution)/shard_map/all_to_all | solution.py:25
  108.7 0.9 shard_map.117
  109.6 0.0 collective-permute-done.5.refs_1_
  109.6 12.4 %all-to-all-start.4 = ((bf16[4,288,128]{2,1,0:T(8,128)(2,1)}), bf16[4,288,128]{2,1,0:T(8,128)(2,1)S(1)}, u32[]{:S(2)}, u32[]{:S(2)}) async-start(bf16[4,288,128]{2,1,0:T(8,128)(2,1)} %shard_map.117), calls=%async_computation.4 | async-start | bytes 589824 | tf_op jit(solution)/shard_map/all_to_all | solution.py:25
  122.0 4.2 %collective-permute-start.6 = (bf16[4,64,256]{2,1,0:T(8,128)(2,1)S(1)}, bf16[4,64,256]{2,1,0:T(8,128)(2,1)S(1)}, u32[]{:S(2)}, u32[]{:S(2)}) collective-permute-start(bf16[4,64,256]{2,1,0:T(8,128)(2,1)S(1)} %get-tuple-element.53), channel_id=1, source_target_pairs={{0,96},{32,0},{64,32},{96,64},{1,97},{33,1},{65,33},{97,65},{2,98}... | collective-permute-start | bytes 393224 | tf_op jit(solution)/shard_map/ppermute | solution.py:227
  126.1 3.0 %collective-permute-start.7 = (bf16[4,64,256]{2,1,0:T(8,128)(2,1)S(1)}, bf16[4,64,256]{2,1,0:T(8,128)(2,1)S(1)}, u32[]{:S(2)}, u32[]{:S(2)}) collective-permute-start(bf16[4,64,256]{2,1,0:T(8,128)(2,1)S(1)} %get-tuple-element.54), channel_id=1, source_target_pairs={{0,64},{32,96},{64,0},{96,32},{1,65},{33,97},{65,1},{97,33},{2,66}... | collective-permute-start | bytes 393224 | tf_op jit(solution)/shard_map/ppermute | solution.py:227
  129.1 0.9 collective-permute-done.6.refs_2_
  130.0 4.5 %collective-permute-done.7.refs_3_ = bf16[4,64,256]{2,1,0:T(8,128)(2,1)S(1)} collective-permute-done((bf16[4,64,256]{2,1,0:T(8,128)(2,1)S(1)}, bf16[4,64,256]{2,1,0:T(8,128)(2,1)S(1)}, u32[]{:S(2)}, u32[]{:S(2)}) %collective-permute-start.7) | collective-permute-done | bytes 131104 | tf_op jit(solution)/shard_map/ppermute | solution.py:227
  134.5 0.1 shard_map.118
  134.6 3.9 %collective-permute-start.10 = (bf16[64,256]{1,0:T(8,128)(2,1)S(1)}, bf16[64,256]{1,0:T(8,128)(2,1)S(1)}, u32[]{:S(2)}, u32[]{:S(2)}) collective-permute-start(bf16[64,256]{1,0:T(8,128)(2,1)S(1)} %get-tuple-element.59), channel_id=1, source_target_pairs={{0,2},{1,3},{2,0},{3,1},{4,6},{5,7},{6,4},{7,5},{8,10},{9,11},{10,... | collective-permute-start | bytes 98312 | tf_op jit(solution)/shard_map/ppermute | solution.py:231
  138.4 2.6 %collective-permute-start.8 = (bf16[64,256]{1,0:T(8,128)(2,1)S(1)}, bf16[64,256]{1,0:T(8,128)(2,1)S(1)}, u32[]{:S(2)}, u32[]{:S(2)}) collective-permute-start(bf16[64,256]{1,0:T(8,128)(2,1)S(1)} %get-tuple-element.56), channel_id=1, source_target_pairs={{0,1},{1,2},{2,3},{3,0},{4,5},{5,6},{6,7},{7,4},{8,9},{9,10},{10,1... | collective-permute-start | bytes 98312 | tf_op jit(solution)/shard_map/ppermute | solution.py:231
  141.0 3.3 %collective-permute-start.9 = (bf16[64,256]{1,0:T(8,128)(2,1)S(1)}, bf16[64,256]{1,0:T(8,128)(2,1)S(1)}, u32[]{:S(2)}, u32[]{:S(2)}) collective-permute-start(bf16[64,256]{1,0:T(8,128)(2,1)S(1)} %get-tuple-element.57), channel_id=1, source_target_pairs={{0,3},{1,0},{2,1},{3,2},{4,7},{5,4},{6,5},{7,6},{8,11},{9,8},{10,9... | collective-permute-start | bytes 98312 | tf_op jit(solution)/shard_map/ppermute | solution.py:231
  144.3 0.0 collective-permute-done.10.refs_3_
  144.3 0.0 all-to-all-done.4.parts_ref
  144.3 0.7 shard_map.120
  145.0 0.0 collective-permute-done.8.refs_1_
  145.0 3.0 %collective-permute-done.9.refs_2_ = bf16[64,256]{1,0:T(8,128)(2,1)S(1)} collective-permute-done((bf16[64,256]{1,0:T(8,128)(2,1)S(1)}, bf16[64,256]{1,0:T(8,128)(2,1)S(1)}, u32[]{:S(2)}, u32[]{:S(2)}) %collective-permute-start.9) | collective-permute-done | bytes 32800 | tf_op jit(solution)/shard_map/ppermute | solution.py:231
  148.0 1.2 shard_map.119
  (9 shorter events, 0.0 us)
Async XLA Ops:
  0.6 0.9 copy-start.2
  2.4 28.6 %all-to-all-start = ((bf16[16,64,256]{2,1,0:T(8,128)(2,1)}), bf16[16,64,256]{2,1,0:T(8,128)(2,1)S(1)}, u32[]{:S(2)}, u32[]{:S(2)}) async-start(bf16[16,64,256]{2,1,0:T(8,128)(2,1)} %shard_map.109), calls=%async_computation | async-start | bytes 1048576 | tf_op jit(solution)/shard_map/all_to_all | solution.py:25
  13.3 11.3 %collective-permute-start.2 = (bf16[256,512]{1,0:T(8,128)(2,1)}, bf16[256,512]{1,0:T(8,128)(2,1)S(1)}, u32[]{:S(2)}, u32[]{:S(2)}) collective-permute-start(bf16[256,512]{1,0:T(8,128)(2,1)} %shard_map.110.refs_0_), channel_id=1, source_target_pairs={{0,1},{1,2},{2,3},{3,0},{4,5},{5,6},{6,7},{7,4},{8,9},{9,10},{10,1... | collective-permute-start | bytes 786440 | tf_op jit(solution)/shard_map/ppermute | solution.py:193
  15.4 12.5 %collective-permute-start.1 = (bf16[256,512]{1,0:T(8,128)(2,1)}, bf16[256,512]{1,0:T(8,128)(2,1)S(1)}, u32[]{:S(2)}, u32[]{:S(2)}) collective-permute-start(bf16[256,512]{1,0:T(8,128)(2,1)} %shard_map.110.refs_0_), channel_id=1, source_target_pairs={{0,2},{1,3},{2,0},{3,1},{4,6},{5,7},{6,4},{7,5},{8,10},{9,11},{10,... | collective-permute-start | bytes 786440 | tf_op jit(solution)/shard_map/ppermute | solution.py:193
  20.0 11.0 %collective-permute-start = (bf16[256,512]{1,0:T(8,128)(2,1)}, bf16[256,512]{1,0:T(8,128)(2,1)S(1)}, u32[]{:S(2)}, u32[]{:S(2)}) collective-permute-start(bf16[256,512]{1,0:T(8,128)(2,1)} %shard_map.110.refs_0_), channel_id=1, source_target_pairs={{0,3},{1,0},{2,1},{3,2},{4,7},{5,4},{6,5},{7,6},{8,11},{9,8},{10,9... | collective-permute-start | bytes 786440 | tf_op jit(solution)/shard_map/ppermute | solution.py:193
  31.0 3.8 %collective-permute-start.3 = (bf16[4,4,64,256]{3,2,1,0:T(8,128)(2,1)S(1)}, bf16[4,4,64,256]{3,2,1,0:T(8,128)(2,1)S(1)}, u32[]{:S(2)}, u32[]{:S(2)}) collective-permute-start(bf16[4,4,64,256]{3,2,1,0:T(8,128)(2,1)S(1)} %bitcast.8), channel_id=1, source_target_pairs={{0,16},{16,0},{1,17},{17,1},{2,18},{18,2},{3,19},{19,3},{4,20},{20... | collective-permute-start | bytes 1572872 | tf_op jit(solution)/shard_map/ppermute | solution.py:198
  34.8 1.0 copy-start
  35.8 25.8 %copy-start.6 = (f32[4096]{0:T(1024)S(1)}, f32[4096]{0:T(1024)}, u32[]{:S(2)}) copy-start(f32[4096]{0:T(1024)} %param.9) | copy-start | bytes 49156
  37.0 24.6 %copy-start.3 = (bf16[16,4096]{1,0:T(8,128)(2,1)S(1)}, bf16[16,4096]{1,0:T(8,128)(2,1)}, u32[]{:S(2)}) copy-start(bf16[16,4096]{1,0:T(8,128)(2,1)} %residual_ref.1) | copy-start | bytes 393220
  37.0 24.6 %copy-start.4 = (bf16[16,4096]{1,0:T(8,128)(2,1)S(1)}, bf16[16,4096]{1,0:T(8,128)(2,1)}, u32[]{:S(2)}) copy-start(bf16[16,4096]{1,0:T(8,128)(2,1)} %upstream_ref.1) | copy-start | bytes 393220
  37.0 24.6 %copy-start.5 = (bf16[16,4096]{1,0:T(8,128)(2,1)S(1)}, bf16[16,4096]{1,0:T(8,128)(2,1)}, u32[]{:S(2)}) copy-start(bf16[16,4096]{1,0:T(8,128)(2,1)} %resid_grad_ref.1) | copy-start | bytes 393220
  90.7 5.0 %copy-start.1 = (bf16[256,512]{1,0:T(8,128)(2,1)S(1)}, bf16[256,512]{1,0:T(8,128)(2,1)}, u32[]{:S(2)}) copy-start(bf16[256,512]{1,0:T(8,128)(2,1)} %shard_map.110.refs_0_) | copy-start | bytes 786436
  90.7 18.0 %all-to-all-start.3 = ((bf16[4,1088,128]{2,1,0:T(8,128)(2,1)}), bf16[4,1088,128]{2,1,0:T(8,128)(2,1)S(1)}, u32[]{:S(2)}, u32[]{:S(2)}) async-start(bf16[4,1088,128]{2,1,0:T(8,128)(2,1)} %shard_map.114), calls=%async_computation.3 | async-start | bytes 2228224 | tf_op jit(solution)/shard_map/all_to_all | solution.py:25
  97.0 3.8 %collective-permute-start.4 = (bf16[4,4,64,256]{3,2,1,0:T(8,128)(2,1)S(1)}, bf16[4,4,64,256]{3,2,1,0:T(8,128)(2,1)S(1)}, u32[]{:S(2)}, u32[]{:S(2)}) collective-permute-start(bf16[4,4,64,256]{3,2,1,0:T(8,128)(2,1)S(1)} %get-tuple-element.48), channel_id=1, source_target_pairs={{0,16},{16,0},{1,17},{17,1},{2,18},{18,2},{3,19},{19,3},{4,20},{20... | collective-permute-start | bytes 1572872 | tf_op jit(solution)/shard_map/ppermute | solution.py:226
  100.9 8.7 %collective-permute-start.5 = (bf16[4,64,256]{2,1,0:T(8,128)(2,1)S(1)}, bf16[4,64,256]{2,1,0:T(8,128)(2,1)S(1)}, u32[]{:S(2)}, u32[]{:S(2)}) collective-permute-start(bf16[4,64,256]{2,1,0:T(8,128)(2,1)S(1)} %get-tuple-element.51), channel_id=1, source_target_pairs={{0,32},{32,64},{64,96},{96,0},{1,33},{33,65},{65,97},{97,1},{2,34}... | collective-permute-start | bytes 393224 | tf_op jit(solution)/shard_map/ppermute | solution.py:227
  109.6 34.7 %all-to-all-start.4 = ((bf16[4,288,128]{2,1,0:T(8,128)(2,1)}), bf16[4,288,128]{2,1,0:T(8,128)(2,1)S(1)}, u32[]{:S(2)}, u32[]{:S(2)}) async-start(bf16[4,288,128]{2,1,0:T(8,128)(2,1)} %shard_map.117), calls=%async_computation.4 | async-start | bytes 589824 | tf_op jit(solution)/shard_map/all_to_all | solution.py:25
  122.0 8.1 %collective-permute-start.6 = (bf16[4,64,256]{2,1,0:T(8,128)(2,1)S(1)}, bf16[4,64,256]{2,1,0:T(8,128)(2,1)S(1)}, u32[]{:S(2)}, u32[]{:S(2)}) collective-permute-start(bf16[4,64,256]{2,1,0:T(8,128)(2,1)S(1)} %get-tuple-element.53), channel_id=1, source_target_pairs={{0,96},{32,0},{64,32},{96,64},{1,97},{33,1},{65,33},{97,65},{2,98}... | collective-permute-start | bytes 393224 | tf_op jit(solution)/shard_map/ppermute | solution.py:227
  126.1 8.4 %collective-permute-start.7 = (bf16[4,64,256]{2,1,0:T(8,128)(2,1)S(1)}, bf16[4,64,256]{2,1,0:T(8,128)(2,1)S(1)}, u32[]{:S(2)}, u32[]{:S(2)}) collective-permute-start(bf16[4,64,256]{2,1,0:T(8,128)(2,1)S(1)} %get-tuple-element.54), channel_id=1, source_target_pairs={{0,64},{32,96},{64,0},{96,32},{1,65},{33,97},{65,1},{97,33},{2,66}... | collective-permute-start | bytes 393224 | tf_op jit(solution)/shard_map/ppermute | solution.py:227
  134.6 9.7 %collective-permute-start.10 = (bf16[64,256]{1,0:T(8,128)(2,1)S(1)}, bf16[64,256]{1,0:T(8,128)(2,1)S(1)}, u32[]{:S(2)}, u32[]{:S(2)}) collective-permute-start(bf16[64,256]{1,0:T(8,128)(2,1)S(1)} %get-tuple-element.59), channel_id=1, source_target_pairs={{0,2},{1,3},{2,0},{3,1},{4,6},{5,7},{6,4},{7,5},{8,10},{9,11},{10,... | collective-permute-start | bytes 98312 | tf_op jit(solution)/shard_map/ppermute | solution.py:231
  138.4 6.6 %collective-permute-start.8 = (bf16[64,256]{1,0:T(8,128)(2,1)S(1)}, bf16[64,256]{1,0:T(8,128)(2,1)S(1)}, u32[]{:S(2)}, u32[]{:S(2)}) collective-permute-start(bf16[64,256]{1,0:T(8,128)(2,1)S(1)} %get-tuple-element.56), channel_id=1, source_target_pairs={{0,1},{1,2},{2,3},{3,0},{4,5},{5,6},{6,7},{7,4},{8,9},{9,10},{10,1... | collective-permute-start | bytes 98312 | tf_op jit(solution)/shard_map/ppermute | solution.py:231
  141.0 7.0 %collective-permute-start.9 = (bf16[64,256]{1,0:T(8,128)(2,1)S(1)}, bf16[64,256]{1,0:T(8,128)(2,1)S(1)}, u32[]{:S(2)}, u32[]{:S(2)}) collective-permute-start(bf16[64,256]{1,0:T(8,128)(2,1)S(1)} %get-tuple-element.57), channel_id=1, source_target_pairs={{0,3},{1,0},{2,1},{3,2},{4,7},{5,4},{6,5},{7,6},{8,11},{9,8},{10,9... | collective-permute-start | bytes 98312 | tf_op jit(solution)/shard_map/ppermute | solution.py:231

commit v3 on v2

--- a/solution.py
+++ b/solution.py
@@ -29,46 +29,70 @@
     return [(i, (i + step) % 4) for i in range(4)]
 
 
-def regroup_kernel(att_ref, out_ref):
+def pieces_kernel(at_ref, att_hbm_ref, weight_ref, out_ref, att_ref, quarter, sems):
+    first = pltpu.make_async_copy(att_hbm_ref, att_ref, sems.at[0])
+    copy = pltpu.make_async_copy(
+        weight_ref.at[pl.ds(pl.multiple_of(at_ref[2] * 64, 64), 64)], quarter, sems.at[1]
+    )
+    first.start()
+    copy.start()
+    first.wait()
     for x in range(4):
         for z in range(4):
             rows = att_ref[z * 64 + x * 16 : z * 64 + x * 16 + 16]
             for y in range(4):
                 out_ref[y * 4 + x, z * 16 : z * 16 + 16] = rows
-
-
-def columns_kernel(yc_ref, weight_ref, out_ref, sems):
-    copies = [
-        pltpu.make_async_copy(
-            weight_ref.at[:, pl.ds(pl.multiple_of(yc_ref[0] * 128 + h * 1024, 128), 128)],
-            out_ref.at[:, h * 128 : h * 128 + 128],
-            sems.at[h],
-        )
-        for h in range(4)
-    ]
-    for copy in copies:
-        copy.start()
-    for copy in copies:
-        copy.wait()
-
-
-def columns(yc, weight):
+    copy.wait()
+    for y in range(4):
+        for h in range(4):
+            start = pl.multiple_of((h * 8 + y * 2 + at_ref[0]) * 128, 128)
+            piece = quarter[:, pl.ds(start, 128)]
+            rows, cols = 64 + h // 2 * 64, h % 2 * 128
+            for x in range(4):
+                out_ref[y * 4 + x, rows : rows + 64, cols : cols + 128] = piece
+
+
+def pieces(at, attention, weight):
     return pl.pallas_call(
-        columns_kernel,
-        out_shape=shape((256, 512)),
-        in_specs=[SCALAR, pl.BlockSpec(memory_space=pl.ANY)],
-        scratch_shapes=[pltpu.SemaphoreType.DMA((4,))],
-    )(yc, weight)
-
-
-def forward_kernel(c_ref, own_ref, other_ref, *refs):
-    c, x = c_ref[0], c_ref[1]
+        pieces_kernel,
+        out_shape=shape((16, 192, 256)),
+        in_specs=[SCALAR] + [pl.BlockSpec(memory_space=pl.ANY)] * 2,
+        scratch_shapes=[
+            pltpu.VMEM((256, 256), BF16),
+            pltpu.VMEM((64, 4096), BF16),
+            pltpu.SemaphoreType.DMA((2,)),
+        ],
+    )(at, attention, weight)
+
+
+def split_kernel(parts_ref, att_ref, weight_ref):
+    att_ref[...] = parts_ref[:, :, :64]
+    for x in range(4):
+        for half in range(2):
+            weight_ref[x * 256 : x * 256 + 256, half * 256 : half * 256 + 256] = parts_ref[
+                :, x, 64 + half * 64 : 128 + half * 64
+            ].reshape(256, 256)
+
+
+def apart(bits):
+    return [(i, i ^ bits) for i in range(4)]
+
+
+def forward_kernel(c_ref, own_ref, other_ref, weight_ref, out_ref):
+    c = c_ref[0]
     for att_ref, core in ((own_ref, c), (other_ref, 1 - c)):
         total = jnp.zeros((256, 512), F32)
-        for j in range(4):
-            att = att_ref[:, lax.rem(x + j, 4)].reshape(256, 256)
-            total += jnp.dot(att, refs[j][...], preferred_element_type=F32)
-        refs[4][pl.ds(core * 16, 16)] = total.astype(BF16).reshape(16, 16, 512)
+        for x in range(4):
+            total += jnp.dot(
+                att_ref[:, x].reshape(256, 256),
+                weight_ref[x * 256 : x * 256 + 256],
+                preferred_element_type=F32,
+            )
+        total = total.astype(BF16)
+        for y in range(4):
+            for z in range(4):
+                at = (y * 4 + z) * 16
+                out_ref[z * 8 + core * 4 + y] = total[at : at + 16]
 
 
 def norm_kernel(
@@ -77,10 +101,10 @@
 ):
     for c in range(2):
         for y in range(4):
-            at = (c * 4 + y) * 4
+            at = c * 4 + y
             total = parts_ref[at].astype(F32)
             for k in range(1, 4):
-                total += parts_ref[at + k].astype(F32)
+                total += parts_ref[at + k * 8].astype(F32)
             for h in range(4):
                 start = (h * 8 + y * 2 + c) * 128
                 projected_ref[:, start : start + 128] = total[:, h * 128 : h * 128 + 128]
@@ -106,14 +130,16 @@
             for h in range(4):
                 start = (h * 8 + y * 2 + c) * 128
                 for z in range(4):
-                    to = (c * 4 + y) * 4 + z
+                    to = (z * 2 + c) * 4 + y
                     cols_ref[to, h * 16 : h * 16 + 16] = grad[:, start : start + 128]
 
 
 def unpack_kernel(parts_ref, grads_ref, gain_ref):
     gain_ref[...] = jnp.sum(parts_ref[:, 64:].astype(F32), axis=0)
-    for h in range(4):
-        grads_ref[:, h * 128 : h * 128 + 128] = parts_ref[:, h * 16 : h * 16 + 16].reshape(512, 128)
+    for k in range(32):
+        at = (k % 8 * 4 + k // 8) * 16
+        for h in range(4):
+            grads_ref[at : at + 16, h * 128 : h * 128 + 128] = parts_ref[k, h * 16 : h * 16 + 16]
 
 
 def weight_kernel(at_ref, own_ref, other_ref, grads_ref, gain_ref, out_ref):
@@ -154,29 +180,42 @@
     gain_ref[...] = total[256:]
 
 
-def back_kernel(at_ref, grads_ref, *refs):
-    for out_ref, core in ((refs[4], 1 - at_ref[0]), (refs[5], at_ref[0])):
+def place(there, here):
+    apart = there ^ here
+    return (apart & 1) * 2 + (apart >> 1)
+
+
+def back_kernel(at_ref, grads_ref, weight_ref, send_ref, keep_ref):
+    for out_ref, core in ((send_ref, 1 - at_ref[0]), (keep_ref, at_ref[0])):
         rows = grads_ref[pl.ds(pl.multiple_of(core * 256, 256), 256)]
         for j in range(4):
+            start = pl.multiple_of(lax.rem(at_ref[1] + j, 4) * 256, 256)
             back = lax.dot_general(
-                rows, refs[j][...], (((1,), (1,)), ((), ())), preferred_element_type=F32
+                rows,
+                weight_ref[pl.ds(start, 256)],
+                (((1,), (1,)), ((), ())),
+                preferred_element_type=F32,
             )
             back = back.reshape(4, 64, 256).astype(out_ref.dtype)
             for y in range(4):
-                out_ref[lax.rem(y + 4 - at_ref[2], 4), j] = back[y]
-
-
-def add_core_kernel(keep_ref, other_ref, *refs):
+                out_ref[place(y, at_ref[2]), j] = back[y]
+
+
+def add_core_kernel(keep_ref, other_ref, stay_ref, go_ref):
+    total = keep_ref[...] + other_ref[...].astype(F32)
+    stay_ref[...] = total[:2]
+    go_ref[...] = total[2:].astype(BF16)
+
+
+def add_y_kernel(keep_ref, other_ref, stay_ref, go_ref):
+    stay_ref[...] = keep_ref[0] + other_ref[0].astype(F32)
+    go_ref[...] = (keep_ref[1] + other_ref[1].astype(F32)).astype(BF16)
+
+
+def add_last_kernel(keep_ref, other_ref, *refs):
+    total = (keep_ref[...] + other_ref[...].astype(F32)).astype(BF16)
     for j in range(4):
-        refs[j][...] = (keep_ref[j] + other_ref[j].astype(F32)).astype(BF16)
-
-
-def add_y_kernel(*refs):
-    total = refs[0][...].astype(F32)
-    for ref in refs[1:4]:
-        total += ref[...].astype(F32)
-    for j in range(4):
-        refs[4 + j][...] = total[j].astype(BF16)
+        refs[j][...] = total[j]
 
 
 def join_kernel(at_ref, *refs):
@@ -189,16 +228,12 @@
     at = jnp.stack([c, x, y])
     swap = [(0, 1), (1, 0)]
 
-    weight = columns((y * 2 + c).reshape(1), out_weight)
-    weights = [weight] + [lax.ppermute(weight, "x", ring(4 - j)) for j in (1, 2, 3)]
-
-    own = call(regroup_kernel, shape((16, 64, 256)), attention)
-    own = a2a(own, ("y", "x")).reshape(4, 4, 64, 256)
-    own, *weights = lax.optimization_barrier((own, *weights))
+    own = a2a(pieces(at, attention, out_weight), ("y", "x")).reshape(4, 4, 192, 256)
+    own, weight = call(split_kernel, (shape((4, 4, 64, 256)), shape((1024, 512))), own)
     other = lax.ppermute(own, "c", swap)
 
-    parts = call(forward_kernel, shape((32, 16, 512)), at, own, other, *weights)
-    parts = a2a(parts, ("c", "y", "zl"))
+    parts = call(forward_kernel, shape((32, 16, 512)), at, own, other, weight)
+    parts = a2a(parts, ("zl", "c", "y"))
 
     normed, stream_out, stream_grad, cols = pl.pallas_call(
         norm_kernel,
@@ -209,11 +244,11 @@
     )(parts, residual, norm_gain.reshape(1, 4096), grad_normed, grad_resid)
 
     grads, gain = call(
-        unpack_kernel, (shape((512, 512)), shape((32, 128), F32)), a2a(cols, ("c", "y", "zl"))
+        unpack_kernel, (shape((512, 512)), shape((32, 128), F32)), a2a(cols, ("zl", "c", "y"))
     )
 
     blocks = call(weight_kernel, shape((4, 1088, 128)), at, own, other, grads, gain)
-    blocks, weights[0] = lax.optimization_barrier((blocks, weights[0]))
+    blocks, weight = lax.optimization_barrier((blocks, weight))
     by_zh = call(weight_x_kernel, shape((4, 288, 128)), a2a(blocks, "x"))
 
     send, keep = call(
@@ -221,13 +256,18 @@
         (shape((4, 4, 64, 256)), shape((4, 4, 64, 256), F32)),
         at,
         grads,
-        *weights,
-    )
-    back = call(add_core_kernel, (shape((4, 64, 256)),) * 4, keep, lax.ppermute(send, "c", swap))
-    moved = [lax.ppermute(back[k], "y", ring(k)) for k in (1, 3, 2)]
-    by_zh, moved[0] = lax.optimization_barrier((by_zh, moved[0]))
+        weight,
+    )
+    half = (2, 4, 64, 256)
+    stay, go = call(
+        add_core_kernel, (shape(half, F32), shape(half)), keep, lax.ppermute(send, "c", swap)
+    )
+    near = lax.ppermute(go, "y", apart(1))
+    by_zh, near = lax.optimization_barrier((by_zh, near))
     parts = a2a(by_zh, "zh")
-    back = call(add_y_kernel, (shape((64, 256)),) * 4, back[0], *moved)
+    stay, go = call(add_y_kernel, (shape(half[1:], F32), shape(half[1:])), stay, near)
+    far = lax.ppermute(go, "y", apart(2))
+    back = call(add_last_kernel, (shape((64, 256)),) * 4, stay, far)
     moved = [lax.ppermute(back[k], "x", ring(k)) for k in (1, 3, 2)]
     parts, moved[2] = lax.optimization_barrier((parts, moved[2]))
     weight_grad, gain = call(

time: 150 us -> 148 us (0.987)
  blocking collectives: 50 us -> 76.6 us
  starting transfers between devices: 58.9 us -> 37.4 us
  waiting for transfers between devices: 25.9 us -> 19.5 us
  local copies, waits for them, and re-layouts: 1.87 us -> 0.02 us
    all_to_all x2 -> x3, blocking collectives: 50 us -> 76.6 us  [a2a(): return lax.all_to_all(value, axes, 0, 0, tiled=True)]
    ppermute x6 -> x2, starting transfers between devices: 18.8 us -> 6.14 us  [the longest x1 3.82 us: local(): far = lax.ppermute(go, 'y', apart(2))]
    ppermute x6 -> x2, waiting for transfers between devices: 14.4 us -> 4.9 us  [the longest x1 4.53 us: local(): far = lax.ppermute(go, 'y', apart(2))]
    all_to_all x3 -> x2, starting transfers between devices: 26.6 us -> 17.9 us  [a2a(): return lax.all_to_all(value, axes, 0, 0, tiled=True)]
    all_to_all x3 -> x2, waiting for transfers between devices: 4.77 us -> 7.88 us  [a2a(): return lax.all_to_all(value, axes, 0, 0, tiled=True)]
    unnamed x14 -> x10, local copies, waits for them, and re-layouts: 1.87 us -> 0.02 us
    pallas_call x10 -> x11, Pallas kernels: 8.66 us -> 7.98 us  [call(): pl.pallas_call(kernel, out_shape=out_shape, in_specs=specs, compiler_para...]
  transfers between devices with their start and end apart: 14 -> 9, of which waited for: 9 -> 7; matrix products, arithmetic and copies ran while one was open for 0% -> 0% of each run, Pallas kernels for 3% -> 2%
where the time goes in v3:
time: 148 us; the launch traced here: 147 us
  blocking collectives  76.6 us (52%)
  starting transfers between devices  37.4 us (25%)
  waiting for transfers between devices  19.5 us (13%)
  Pallas kernels  12.4 us (8%)
    all_to_all x3, blocking collectives, a2a(): return lax.all_to_all(value, axes, 0, 0, tiled=True)  76.6 us
    all_to_all x2, starting transfers between devices, a2a(): return lax.all_to_all(value, axes, 0, 0, tiled=True)  17.9 us
    ppermute x3, starting transfers between devices, local(): moved = [lax.ppermute(back[k], 'x', ring(k)) for k in (1, 3, 2)]  9.46 us
    pallas_call x11, Pallas kernels, call(): pl.pallas_call(kernel, out_shape=out_shape, in_specs=specs, compiler_para...  7.98 us
    all_to_all x2, waiting for transfers between devices, a2a(): return lax.all_to_all(value, axes, 0, 0, tiled=True)  7.88 us
    ppermute x1, waiting for transfers between devices, local(): far = lax.ppermute(go, 'y', apart(2))  4.53 us
    ppermute x1, starting transfers between devices, local(): far = lax.ppermute(go, 'y', apart(2))  3.82 us
    pallas_call x1, Pallas kernels, pieces(): pl.pallas_call(pieces_kernel, out_shape=shape((16, 192, 256)), in_specs=[...  3.09 us
  transfers between devices with their start and end apart: 9, of which 7 were waited for; matrix products, arithmetic and copies ran while one was open for 0% of the time, Pallas kernels for 2%

profile of v3, /device:TPU:6, one launch (start us, length us, event | category | flops | bytes accessed | tf_op | source)
XLA Modules:
  0.0 147.3 jit_solution(7959531283555702851)
XLA Ops:
  0.6 0.6 pad_add_fusion.at_ref.c_ref
  1.2 3.1 %shard_map.109 = bf16[16,192,256]{2,1,0:T(8,128)(2,1)} custom-call(s32[3]{0:T(128)} %pad_add_fusion.at_ref.c_ref, bf16[256,256]{1,0:T(8,128)(2,1)} %att_hbm_ref.1, bf16[256,4096]{1,0:T(8,128)(2,1)} %weight_ref.1), custom_call_target="tpu_custom_call" | custom-call | tf_op jit(solution)/shard_map/pallas_call | solution.py:56
  4.3 27.6 %all_to_all.25 = bf16[16,192,256]{2,1,0:T(8,128)(2,1)S(1)} all-to-all(bf16[16,192,256]{2,1,0:T(8,128)(2,1)} %shard_map.109), channel_id=1, replica_groups=mesh['zh'=4,'y'=4,'c'=2,'zl'=4,'x'=4] {'y','x'}, dimensions={0} | all-to-all | bytes 3145728 | tf_op jit(solution)/shard_map/all_to_all | solution.py:25
  31.9 0.0 copy-start.3
  31.9 0.1 shard_map.110
  32.0 1.9 %collective-permute-start = (bf16[4,4,64,256]{3,2,1,0:T(8,128)(2,1)S(1)}, bf16[4,4,64,256]{3,2,1,0:T(8,128)(2,1)S(1)}, u32[]{:S(2)}, u32[]{:S(2)}) collective-permute-start(bf16[4,4,64,256]{3,2,1,0:T(8,128)(2,1)S(1)} %get-tuple-element.32.own_ref), channel_id=1, source_target_pairs={{0,16},{16,0},{1,17},{17,1},{2,18},{18,2},{3,19},{19,3},{4,20},{20... | collective-permute-start | bytes 1572872 | tf_op jit(solution)/shard_map/ppermute | solution.py:233
  33.9 1.9 %collective-permute-done.other_ref = bf16[4,4,64,256]{3,2,1,0:T(8,128)(2,1)S(1)} collective-permute-done((bf16[4,4,64,256]{3,2,1,0:T(8,128)(2,1)S(1)}, bf16[4,4,64,256]{3,2,1,0:T(8,128)(2,1)S(1)}, u32[]{:S(2)}, u32[]{:S(2)}) %collective-permute-start) | collective-permute-done | bytes 524320 | tf_op jit(solution)/shard_map/ppermute | solution.py:233
  35.8 0.0 copy-done.3
  35.8 0.0 copy-start
  35.8 0.0 copy-start.1
  35.8 0.0 copy-start.2
  35.8 0.0 copy-start.4
  35.8 1.2 shard_map.111
  37.1 23.6 %all_to_all.26.parts_ref = bf16[32,16,512]{2,1,0:T(8,128)(2,1)S(1)} all-to-all(bf16[32,16,512]{2,1,0:T(8,128)(2,1)S(1)} %shard_map.111), channel_id=1, replica_groups=mesh['zh'=4,'y'=4,'c'=2,'zl'=4,'x'=4] {'zl','c','y'}, dimensions={0} | all-to-all | bytes 1048576 | tf_op jit(solution)/shard_map/all_to_all | solution.py:25
  60.7 0.0 copy-done
  60.7 0.0 copy-done.1
  60.7 0.0 copy-done.2
  60.7 0.0 copy-done.4
  60.7 1.3 shard_map.112
  62.0 25.5 %all_to_all.27.parts_ref = bf16[32,96,128]{2,1,0:T(8,128)(2,1)S(1)} all-to-all(bf16[32,96,128]{2,1,0:T(8,128)(2,1)S(1)} %get-tuple-element.37), channel_id=1, replica_groups=mesh['zh'=4,'y'=4,'c'=2,'zl'=4,'x'=4] {'zl','c','y'}, dimensions={0} | all-to-all | bytes 1572864 | tf_op jit(solution)/shard_map/all_to_all | solution.py:25
  87.5 0.1 shard_map.113
  87.6 2.3 %shard_map.114 = bf16[4,1088,128]{2,1,0:T(8,128)(2,1)} custom-call(s32[3]{0:T(128)S(1)} %copy-done.3, bf16[4,4,64,256]{3,2,1,0:T(8,128)(2,1)S(1)} %get-tuple-element.32.own_ref, bf16[4,4,64,256]{3,2,1,0:T(8,128)(2,1)S(1)} %collective-permute-done.other_ref, bf16[512,512]{1,0:T(8,128)(2,1)S(1)} %get-tuple-element.38.grads_ref, ...), custom_call_target="tpu_custom_call" | custom-call | tf_op jit(solution)/shard_map/pallas_call | solution.py:21
  89.9 5.6 %all-to-all-start.3 = ((bf16[4,1088,128]{2,1,0:T(8,128)(2,1)}), bf16[4,1088,128]{2,1,0:T(8,128)(2,1)S(1)}, u32[]{:S(2)}, u32[]{:S(2)}) async-start(bf16[4,1088,128]{2,1,0:T(8,128)(2,1)} %shard_map.114), calls=%async_computation.3 | async-start | bytes 2228224 | tf_op jit(solution)/shard_map/all_to_all | solution.py:25
  95.5 1.3 shard_map.115
  96.8 1.9 %collective-permute-start.1 = (bf16[4,4,64,256]{3,2,1,0:T(8,128)(2,1)S(1)}, bf16[4,4,64,256]{3,2,1,0:T(8,128)(2,1)S(1)}, u32[]{:S(2)}, u32[]{:S(2)}) collective-permute-start(bf16[4,4,64,256]{3,2,1,0:T(8,128)(2,1)S(1)} %get-tuple-element.42), channel_id=1, source_target_pairs={{0,16},{16,0},{1,17},{17,1},{2,18},{18,2},{3,19},{19,3},{4,20},{20... | collective-permute-start | bytes 1572872 | tf_op jit(solution)/shard_map/ppermute | solution.py:263
  98.7 1.9 %collective-permute-done.1.other_ref = bf16[4,4,64,256]{3,2,1,0:T(8,128)(2,1)S(1)} collective-permute-done((bf16[4,4,64,256]{3,2,1,0:T(8,128)(2,1)S(1)}, bf16[4,4,64,256]{3,2,1,0:T(8,128)(2,1)S(1)}, u32[]{:S(2)}, u32[]{:S(2)}) %collective-permute-start.1) | collective-permute-done | bytes 524320 | tf_op jit(solution)/shard_map/ppermute | solution.py:263
  100.6 0.1 shard_map.116
  100.7 2.3 %collective-permute-start.2 = (bf16[2,4,64,256]{3,2,1,0:T(8,128)(2,1)S(1)}, bf16[2,4,64,256]{3,2,1,0:T(8,128)(2,1)S(1)}, u32[]{:S(2)}, u32[]{:S(2)}) collective-permute-start(bf16[2,4,64,256]{3,2,1,0:T(8,128)(2,1)S(1)} %get-tuple-element.45), channel_id=1, source_target_pairs={{0,32},{32,0},{64,96},{96,64},{1,33},{33,1},{65,97},{97,65},{2,34}... | collective-permute-start | bytes 786440 | tf_op jit(solution)/shard_map/ppermute | solution.py:265
  103.0 6.7 %all-to-all-done.3.parts_ref = bf16[4,1088,128]{2,1,0:T(8,128)(2,1)S(1)} async-done(((bf16[4,1088,128]{2,1,0:T(8,128)(2,1)}), bf16[4,1088,128]{2,1,0:T(8,128)(2,1)S(1)}, u32[]{:S(2)}, u32[]{:S(2)}) %all-to-all-start.3) | async-done | bytes 1114144 | tf_op jit(solution)/shard_map/all_to_all | solution.py:25
  109.7 0.9 shard_map.117
  110.6 0.4 collective-permute-done.2.other_ref
  110.9 12.4 %all-to-all-start.4 = ((bf16[4,288,128]{2,1,0:T(8,128)(2,1)}), bf16[4,288,128]{2,1,0:T(8,128)(2,1)S(1)}, u32[]{:S(2)}, u32[]{:S(2)}) async-start(bf16[4,288,128]{2,1,0:T(8,128)(2,1)} %shard_map.117), calls=%async_computation.4 | async-start | bytes 589824 | tf_op jit(solution)/shard_map/all_to_all | solution.py:25
  123.4 3.8 %collective-permute-start.3 = (bf16[4,64,256]{2,1,0:T(8,128)(2,1)S(1)}, bf16[4,64,256]{2,1,0:T(8,128)(2,1)S(1)}, u32[]{:S(2)}, u32[]{:S(2)}) collective-permute-start(bf16[4,64,256]{2,1,0:T(8,128)(2,1)S(1)} %get-tuple-element.48), channel_id=1, source_target_pairs={{0,64},{32,96},{64,0},{96,32},{1,65},{33,97},{65,1},{97,33},{2,66}... | collective-permute-start | bytes 393224 | tf_op jit(solution)/shard_map/ppermute | solution.py:269
  127.2 4.5 %collective-permute-done.3.other_ref = bf16[4,64,256]{2,1,0:T(8,128)(2,1)S(1)} collective-permute-done((bf16[4,64,256]{2,1,0:T(8,128)(2,1)S(1)}, bf16[4,64,256]{2,1,0:T(8,128)(2,1)S(1)}, u32[]{:S(2)}, u32[]{:S(2)}) %collective-permute-start.3) | collective-permute-done | bytes 131104 | tf_op jit(solution)/shard_map/ppermute | solution.py:269
  131.8 3.6 %collective-permute-start.6 = (bf16[64,256]{1,0:T(8,128)(2,1)S(1)}, bf16[64,256]{1,0:T(8,128)(2,1)S(1)}, u32[]{:S(2)}, u32[]{:S(2)}) collective-permute-start(bf16[64,256]{1,0:T(8,128)(2,1)S(1)} %get-tuple-element.53), channel_id=1, source_target_pairs={{0,2},{1,3},{2,0},{3,1},{4,6},{5,7},{6,4},{7,5},{8,10},{9,11},{10,... | collective-permute-start | bytes 98312 | tf_op jit(solution)/shard_map/ppermute | solution.py:271
  135.4 3.7 %collective-permute-start.4 = (bf16[64,256]{1,0:T(8,128)(2,1)S(1)}, bf16[64,256]{1,0:T(8,128)(2,1)S(1)}, u32[]{:S(2)}, u32[]{:S(2)}) collective-permute-start(bf16[64,256]{1,0:T(8,128)(2,1)S(1)} %get-tuple-element.50), channel_id=1, source_target_pairs={{0,1},{1,2},{2,3},{3,0},{4,5},{5,6},{6,7},{7,4},{8,9},{9,10},{10,1... | collective-permute-start | bytes 98312 | tf_op jit(solution)/shard_map/ppermute | solution.py:271
  139.1 2.1 %collective-permute-start.5 = (bf16[64,256]{1,0:T(8,128)(2,1)S(1)}, bf16[64,256]{1,0:T(8,128)(2,1)S(1)}, u32[]{:S(2)}, u32[]{:S(2)}) collective-permute-start(bf16[64,256]{1,0:T(8,128)(2,1)S(1)} %get-tuple-element.51), channel_id=1, source_target_pairs={{0,3},{1,0},{2,1},{3,2},{4,7},{5,4},{6,5},{7,6},{8,11},{9,8},{10,9... | collective-permute-start | bytes 98312 | tf_op jit(solution)/shard_map/ppermute | solution.py:271
  141.2 0.0 collective-permute-done.6.refs_3_
  141.2 1.2 all-to-all-done.4.parts_ref
  142.4 0.7 shard_map.121
  143.1 0.0 collective-permute-done.4.refs_1_
  143.1 3.0 %collective-permute-done.5.refs_2_ = bf16[64,256]{1,0:T(8,128)(2,1)S(1)} collective-permute-done((bf16[64,256]{1,0:T(8,128)(2,1)S(1)}, bf16[64,256]{1,0:T(8,128)(2,1)S(1)}, u32[]{:S(2)}, u32[]{:S(2)}) %collective-permute-start.5) | collective-permute-done | bytes 32800 | tf_op jit(solution)/shard_map/ppermute | solution.py:271
  146.1 1.2 shard_map.120
  (2 shorter events, 0.1 us)
Async XLA Ops:
  31.9 3.9 %copy-start.3 = (s32[3]{0:T(128)S(1)}, s32[3]{0:T(128)}, u32[]{:S(2)}) copy-start(s32[3]{0:T(128)} %pad_add_fusion.at_ref.c_ref) | copy-start | bytes 40
  32.0 3.8 %collective-permute-start = (bf16[4,4,64,256]{3,2,1,0:T(8,128)(2,1)S(1)}, bf16[4,4,64,256]{3,2,1,0:T(8,128)(2,1)S(1)}, u32[]{:S(2)}, u32[]{:S(2)}) collective-permute-start(bf16[4,4,64,256]{3,2,1,0:T(8,128)(2,1)S(1)} %get-tuple-element.32.own_ref), channel_id=1, source_target_pairs={{0,16},{16,0},{1,17},{17,1},{2,18},{18,2},{3,19},{19,3},{4,20},{20... | collective-permute-start | bytes 1572872 | tf_op jit(solution)/shard_map/ppermute | solution.py:233
  35.8 24.9 %copy-start = (bf16[16,4096]{1,0:T(8,128)(2,1)S(1)}, bf16[16,4096]{1,0:T(8,128)(2,1)}, u32[]{:S(2)}) copy-start(bf16[16,4096]{1,0:T(8,128)(2,1)} %residual_ref.1) | copy-start | bytes 393220
  35.8 24.9 %copy-start.1 = (bf16[16,4096]{1,0:T(8,128)(2,1)S(1)}, bf16[16,4096]{1,0:T(8,128)(2,1)}, u32[]{:S(2)}) copy-start(bf16[16,4096]{1,0:T(8,128)(2,1)} %upstream_ref.1) | copy-start | bytes 393220
  35.8 24.9 %copy-start.2 = (bf16[16,4096]{1,0:T(8,128)(2,1)S(1)}, bf16[16,4096]{1,0:T(8,128)(2,1)}, u32[]{:S(2)}) copy-start(bf16[16,4096]{1,0:T(8,128)(2,1)} %resid_grad_ref.1) | copy-start | bytes 393220
  35.8 24.9 %copy-start.4 = (f32[4096]{0:T(1024)S(1)}, f32[4096]{0:T(1024)}, u32[]{:S(2)}) copy-start(f32[4096]{0:T(1024)} %param.9) | copy-start | bytes 49156
  89.9 19.8 %all-to-all-start.3 = ((bf16[4,1088,128]{2,1,0:T(8,128)(2,1)}), bf16[4,1088,128]{2,1,0:T(8,128)(2,1)S(1)}, u32[]{:S(2)}, u32[]{:S(2)}) async-start(bf16[4,1088,128]{2,1,0:T(8,128)(2,1)} %shard_map.114), calls=%async_computation.3 | async-start | bytes 2228224 | tf_op jit(solution)/shard_map/all_to_all | solution.py:25
  96.8 3.8 %collective-permute-start.1 = (bf16[4,4,64,256]{3,2,1,0:T(8,128)(2,1)S(1)}, bf16[4,4,64,256]{3,2,1,0:T(8,128)(2,1)S(1)}, u32[]{:S(2)}, u32[]{:S(2)}) collective-permute-start(bf16[4,4,64,256]{3,2,1,0:T(8,128)(2,1)S(1)} %get-tuple-element.42), channel_id=1, source_target_pairs={{0,16},{16,0},{1,17},{17,1},{2,18},{18,2},{3,19},{19,3},{4,20},{20... | collective-permute-start | bytes 1572872 | tf_op jit(solution)/shard_map/ppermute | solution.py:263
  100.7 10.2 %collective-permute-start.2 = (bf16[2,4,64,256]{3,2,1,0:T(8,128)(2,1)S(1)}, bf16[2,4,64,256]{3,2,1,0:T(8,128)(2,1)S(1)}, u32[]{:S(2)}, u32[]{:S(2)}) collective-permute-start(bf16[2,4,64,256]{3,2,1,0:T(8,128)(2,1)S(1)} %get-tuple-element.45), channel_id=1, source_target_pairs={{0,32},{32,0},{64,96},{96,64},{1,33},{33,1},{65,97},{97,65},{2,34}... | collective-permute-start | bytes 786440 | tf_op jit(solution)/shard_map/ppermute | solution.py:265
  110.9 31.5 %all-to-all-start.4 = ((bf16[4,288,128]{2,1,0:T(8,128)(2,1)}), bf16[4,288,128]{2,1,0:T(8,128)(2,1)S(1)}, u32[]{:S(2)}, u32[]{:S(2)}) async-start(bf16[4,288,128]{2,1,0:T(8,128)(2,1)} %shard_map.117), calls=%async_computation.4 | async-start | bytes 589824 | tf_op jit(solution)/shard_map/all_to_all | solution.py:25
  123.4 8.4 %collective-permute-start.3 = (bf16[4,64,256]{2,1,0:T(8,128)(2,1)S(1)}, bf16[4,64,256]{2,1,0:T(8,128)(2,1)S(1)}, u32[]{:S(2)}, u32[]{:S(2)}) collective-permute-start(bf16[4,64,256]{2,1,0:T(8,128)(2,1)S(1)} %get-tuple-element.48), channel_id=1, source_target_pairs={{0,64},{32,96},{64,0},{96,32},{1,65},{33,97},{65,1},{97,33},{2,66}... | collective-permute-start | bytes 393224 | tf_op jit(solution)/shard_map/ppermute | solution.py:269
  131.8 9.5 %collective-permute-start.6 = (bf16[64,256]{1,0:T(8,128)(2,1)S(1)}, bf16[64,256]{1,0:T(8,128)(2,1)S(1)}, u32[]{:S(2)}, u32[]{:S(2)}) collective-permute-start(bf16[64,256]{1,0:T(8,128)(2,1)S(1)} %get-tuple-element.53), channel_id=1, source_target_pairs={{0,2},{1,3},{2,0},{3,1},{4,6},{5,7},{6,4},{7,5},{8,10},{9,11},{10,... | collective-permute-start | bytes 98312 | tf_op jit(solution)/shard_map/ppermute | solution.py:271
  135.4 7.8 %collective-permute-start.4 = (bf16[64,256]{1,0:T(8,128)(2,1)S(1)}, bf16[64,256]{1,0:T(8,128)(2,1)S(1)}, u32[]{:S(2)}, u32[]{:S(2)}) collective-permute-start(bf16[64,256]{1,0:T(8,128)(2,1)S(1)} %get-tuple-element.50), channel_id=1, source_target_pairs={{0,1},{1,2},{2,3},{3,0},{4,5},{5,6},{6,7},{7,4},{8,9},{9,10},{10,1... | collective-permute-start | bytes 98312 | tf_op jit(solution)/shard_map/ppermute | solution.py:271
  139.1 7.0 %collective-permute-start.5 = (bf16[64,256]{1,0:T(8,128)(2,1)S(1)}, bf16[64,256]{1,0:T(8,128)(2,1)S(1)}, u32[]{:S(2)}, u32[]{:S(2)}) collective-permute-start(bf16[64,256]{1,0:T(8,128)(2,1)S(1)} %get-tuple-element.51), channel_id=1, source_target_pairs={{0,3},{1,0},{2,1},{3,2},{4,7},{5,4},{6,5},{7,6},{8,11},{9,8},{10,9... | collective-permute-start | bytes 98312 | tf_op jit(solution)/shard_map/ppermute | solution.py:271

commit v4 on v3

--- a/solution.py
+++ b/solution.py
@@ -29,40 +29,52 @@
     return [(i, (i + step) % 4) for i in range(4)]
 
 
-def pieces_kernel(at_ref, att_hbm_ref, weight_ref, out_ref, att_ref, quarter, sems):
+def pieces_kernel(att_hbm_ref, weight_ref, out_ref, att_ref, quarter, rows, cols, sems):
+    y, c = lax.axis_index("y"), lax.axis_index("c")
     first = pltpu.make_async_copy(att_hbm_ref, att_ref, sems.at[0])
     copy = pltpu.make_async_copy(
-        weight_ref.at[pl.ds(pl.multiple_of(at_ref[2] * 64, 64), 64)], quarter, sems.at[1]
+        weight_ref.at[pl.ds(pl.multiple_of(y * 64, 64), 64)], quarter, sems.at[1]
     )
     first.start()
     copy.start()
     first.wait()
     for x in range(4):
         for z in range(4):
-            rows = att_ref[z * 64 + x * 16 : z * 64 + x * 16 + 16]
-            for y in range(4):
-                out_ref[y * 4 + x, z * 16 : z * 16 + 16] = rows
+            rows[x, z * 16 : z * 16 + 16] = att_ref[z * 64 + x * 16 : z * 64 + x * 16 + 16]
+    copies = [
+        pltpu.make_async_copy(rows, out_ref.at[y * 4 : y * 4 + 4, :64], sems.at[2 + y])
+        for y in range(4)
+    ]
+    for one in copies:
+        one.start()
     copy.wait()
-    for y in range(4):
+    for there in range(4):
         for h in range(4):
-            start = pl.multiple_of((h * 8 + y * 2 + at_ref[0]) * 128, 128)
-            piece = quarter[:, pl.ds(start, 128)]
-            rows, cols = 64 + h // 2 * 64, h % 2 * 128
-            for x in range(4):
-                out_ref[y * 4 + x, rows : rows + 64, cols : cols + 128] = piece
-
-
-def pieces(at, attention, weight):
+            start = pl.multiple_of((h * 8 + there * 2 + c) * 128, 128)
+            at, to = h // 2 * 64, h % 2 * 128
+            cols[there, at : at + 64, to : to + 128] = quarter[:, pl.ds(start, 128)]
+        for x in range(4):
+            to_ref = out_ref.at[there * 4 + x, 64:]
+            copies.append(pltpu.make_async_copy(cols.at[there], to_ref, sems.at[6 + there * 4 + x]))
+            copies[-1].start()
+    for one in copies:
+        one.wait()
+
+
+def pieces(attention, weight):
     return pl.pallas_call(
         pieces_kernel,
         out_shape=shape((16, 192, 256)),
-        in_specs=[SCALAR] + [pl.BlockSpec(memory_space=pl.ANY)] * 2,
+        in_specs=[pl.BlockSpec(memory_space=pl.ANY)] * 2,
+        out_specs=pl.BlockSpec(memory_space=pl.ANY),
         scratch_shapes=[
             pltpu.VMEM((256, 256), BF16),
             pltpu.VMEM((64, 4096), BF16),
-            pltpu.SemaphoreType.DMA((2,)),
+            pltpu.VMEM((4, 64, 256), BF16),
+            pltpu.VMEM((4, 128, 256), BF16),
+            pltpu.SemaphoreType.DMA((22,)),
         ],
-    )(at, attention, weight)
+    )(attention, weight)
 
 
 def split_kernel(parts_ref, att_ref, weight_ref):
@@ -123,8 +135,11 @@
     grad = (resid_grad_ref[...].astype(F32) + inv_rms * (scaled - unit_rows * inner)).astype(BF16)
     grad_ref[...] = grad
     for k in range(32):
-        rows = jnp.broadcast_to(gain_grad[:, k * 128 : k * 128 + 128], (32, 128))
-        cols_ref[:, 64 + k : 65 + k] = rows.astype(BF16)[:, None]
+        rows = gain_grad[:, k * 128 : k * 128 + 128].astype(BF16)
+        rows = jnp.broadcast_to(rows[None], (4, 1, 128))
+        for z in range(4):
+            to = (z * 2 + k % 2) * 4
+            cols_ref[to : to + 4, 64 + k // 2 : 65 + k // 2] = rows
     for c in range(2):
         for y in range(4):
             for h in range(4):
@@ -159,8 +174,8 @@
         total = total.astype(BF16)
         for h in range(4):
             out_ref[x, h * 256 : h * 256 + 256] = total[:, h * 128 : h * 128 + 128]
-        out_ref[x, 1024:1056] = upper
-        out_ref[x, 1056:] = lower
+        out_ref[x, 1024:1040] = upper
+        out_ref[x, 1040:] = lower
 
 
 def weight_x_kernel(parts_ref, out_ref):
@@ -169,7 +184,7 @@
         total += parts_ref[k].astype(F32)
     for h in range(4):
         out_ref[h, :256] = total[h * 256 : h * 256 + 256].astype(BF16)
-        out_ref[h, 256:] = (total[1024:1056] + total[1056:]).astype(BF16)
+        out_ref[h, 256:] = (total[1024:1040] + total[1040:]).astype(BF16)
 
 
 def weight_zh_kernel(parts_ref, weight_ref, gain_ref):
@@ -218,7 +233,12 @@
         refs[j][...] = total[j]
 
 
-def join_kernel(at_ref, *refs):
+def join_kernel(at_ref, gain_ref, other_ref, *refs):
+    ours, gain, other = at_ref[0] == 0, gain_ref[...], other_ref[...]
+    first, last = jnp.where(ours, gain, other), jnp.where(ours, other, gain)
+    for k in range(16):
+        refs[5][2 * k : 2 * k + 1] = first[k : k + 1]
+        refs[5][2 * k + 1 : 2 * k + 2] = last[k : k + 1]
     for ref, step in zip(refs[:4], (0, 3, 1, 2)):
         refs[4][:, lax.rem(at_ref[1] + step, 4)] = ref[...].reshape(4, 16, 256)
 
@@ -228,7 +248,7 @@
     at = jnp.stack([c, x, y])
     swap = [(0, 1), (1, 0)]
 
-    own = a2a(pieces(at, attention, out_weight), ("y", "x")).reshape(4, 4, 192, 256)
+    own = a2a(pieces(attention, out_weight), ("y", "x")).reshape(4, 4, 192, 256)
     own, weight = call(split_kernel, (shape((4, 4, 64, 256)), shape((1024, 512))), own)
     other = lax.ppermute(own, "c", swap)
 
@@ -237,19 +257,19 @@
 
     normed, stream_out, stream_grad, cols = pl.pallas_call(
         norm_kernel,
-        out_shape=(shape((16, 4096)),) * 3 + (shape((32, 96, 128)),),
+        out_shape=(shape((16, 4096)),) * 3 + (shape((32, 80, 128)),),
         in_specs=[WHOLE] * 5,
         scratch_shapes=[pltpu.VMEM((16, 4096), F32)],
         compiler_params=PARAMS,
     )(parts, residual, norm_gain.reshape(1, 4096), grad_normed, grad_resid)
 
     grads, gain = call(
-        unpack_kernel, (shape((512, 512)), shape((32, 128), F32)), a2a(cols, ("zl", "c", "y"))
-    )
-
-    blocks = call(weight_kernel, shape((4, 1088, 128)), at, own, other, grads, gain)
+        unpack_kernel, (shape((512, 512)), shape((16, 128), F32)), a2a(cols, ("zl", "c", "y"))
+    )
+
+    blocks = call(weight_kernel, shape((4, 1056, 128)), at, own, other, grads, gain)
     blocks, weight = lax.optimization_barrier((blocks, weight))
-    by_zh = call(weight_x_kernel, shape((4, 288, 128)), a2a(blocks, "x"))
+    by_zh = call(weight_x_kernel, shape((4, 272, 128)), a2a(blocks, "x"))
 
     send, keep = call(
         back_kernel,
@@ -271,10 +291,19 @@
     moved = [lax.ppermute(back[k], "x", ring(k)) for k in (1, 3, 2)]
     parts, moved[2] = lax.optimization_barrier((parts, moved[2]))
     weight_grad, gain = call(
-        weight_zh_kernel, (shape((256, 128), F32), shape((32, 128), F32)), parts
-    )
-    attn_grad = call(join_kernel, shape((4, 4, 16, 256)), at, back[0], *moved).reshape(256, 256)
-    return (normed, stream_out, stream_grad, attn_grad, weight_grad, gain.reshape(4096))
+        weight_zh_kernel, (shape((256, 128), F32), shape((16, 128), F32)), parts
+    )
+    attn_grad, gain_grad = call(
+        join_kernel,
+        (shape((4, 4, 16, 256)), shape((32, 128), F32)),
+        at,
+        gain,
+        lax.ppermute(gain, "c", swap),
+        back[0],
+        *moved,
+    )
+    attn_grad, gain_grad = attn_grad.reshape(256, 256), gain_grad.reshape(4096)
+    return (normed, stream_out, stream_grad, attn_grad, weight_grad, gain_grad)
 
 
 def solution(mesh):

time: 148 us -> 146 us (0.986)
  the two profiles are of different devices: /device:TPU:6 before, /device:TPU:1 now
where the time goes in v4:
time: 146 us
  blocking collectives  72.9 us (50%)
  starting transfers between devices  43.9 us (30%)
  waiting for transfers between devices  16.6 us (11%)
  Pallas kernels  11.4 us (8%)
    all_to_all x3, blocking collectives, a2a(): return lax.all_to_all(value, axes, 0, 0, tiled=True)  72.9 us
    all_to_all x2, starting transfers between devices, a2a(): return lax.all_to_all(value, axes, 0, 0, tiled=True)  15.6 us
    ppermute x3, starting transfers between devices, local(): moved = [lax.ppermute(back[k], 'x', ring(k)) for k in (1, 3, 2)]  10.3 us
    pallas_call x11, Pallas kernels, call(): pl.pallas_call(kernel, out_shape=out_shape, in_specs=specs, compiler_para...  7.98 us
    all_to_all x2, waiting for transfers between devices, a2a(): return lax.all_to_all(value, axes, 0, 0, tiled=True)  7.94 us
    ppermute x1, starting transfers between devices, local(): other = lax.ppermute(own, 'c', swap)  6.08 us
    ppermute x1, starting transfers between devices, local(): lax.ppermute(gain, 'c', swap)  5.37 us
    ppermute x1, waiting for transfers between devices, local(): far = lax.ppermute(go, 'y', apart(2))  4.97 us
  transfers between devices with their start and end apart: 10, of which 5 were waited for; matrix products, arithmetic and copies ran while one was open for 0% of the time, Pallas kernels for 2%

profile of v4, /device:TPU:1, one launch (start us, length us, event | category | flops | bytes accessed | tf_op | source)
XLA Modules:
  0.0 145.8 jit_solution(12229666610996260912)
XLA Ops:
  0.6 2.3 %shard_map.109 = bf16[16,192,256]{2,1,0:T(8,128)(2,1)} custom-call(bf16[256,256]{1,0:T(8,128)(2,1)} %att_hbm_ref.1, bf16[256,4096]{1,0:T(8,128)(2,1)} %weight_ref.1), custom_call_target="tpu_custom_call" | custom-call | tf_op jit(solution)/shard_map/pallas_call | solution.py:65
  3.0 27.3 %all_to_all.25 = bf16[16,192,256]{2,1,0:T(8,128)(2,1)S(1)} all-to-all(bf16[16,192,256]{2,1,0:T(8,128)(2,1)} %shard_map.109), channel_id=1, replica_groups=mesh['zh'=4,'y'=4,'c'=2,'zl'=4,'x'=4] {'y','x'}, dimensions={0} | all-to-all | bytes 3145728 | tf_op jit(solution)/shard_map/all_to_all | solution.py:25
  30.2 0.1 shard_map.110
  30.3 6.1 %collective-permute-start = (bf16[4,4,64,256]{3,2,1,0:T(8,128)(2,1)S(1)}, bf16[4,4,64,256]{3,2,1,0:T(8,128)(2,1)S(1)}, u32[]{:S(2)}, u32[]{:S(2)}) collective-permute-start(bf16[4,4,64,256]{3,2,1,0:T(8,128)(2,1)S(1)} %get-tuple-element.34.own_ref), channel_id=1, source_target_pairs={{0,16},{16,0},{1,17},{17,1},{2,18},{18,2},{3,19},{19,3},{4,20},{20... | collective-permute-start | bytes 1572872 | tf_op jit(solution)/shard_map/ppermute | solution.py:253
  36.4 0.1 pad_add_fusion.c_ref.at_ref
  36.5 1.4 collective-permute-done.other_ref
  37.9 0.0 copy-start
  37.9 0.0 copy-start.1
  37.9 0.0 copy-start.2
  38.0 0.0 copy-start.3
  38.0 1.2 shard_map.111
  39.2 22.8 %all_to_all.26.parts_ref = bf16[32,16,512]{2,1,0:T(8,128)(2,1)S(1)} all-to-all(bf16[32,16,512]{2,1,0:T(8,128)(2,1)S(1)} %shard_map.111), channel_id=1, replica_groups=mesh['zh'=4,'y'=4,'c'=2,'zl'=4,'x'=4] {'zl','c','y'}, dimensions={0} | all-to-all | bytes 1048576 | tf_op jit(solution)/shard_map/all_to_all | solution.py:25
  62.0 0.0 copy-done
  62.0 0.0 copy-done.1
  62.0 0.0 copy-done.2
  62.0 0.0 copy-done.3
  62.0 1.1 shard_map.112
  63.1 22.9 %all_to_all.27.parts_ref = bf16[32,80,128]{2,1,0:T(8,128)(2,1)S(1)} all-to-all(bf16[32,80,128]{2,1,0:T(8,128)(2,1)S(1)} %get-tuple-element.39), channel_id=1, replica_groups=mesh['zh'=4,'y'=4,'c'=2,'zl'=4,'x'=4] {'zl','c','y'}, dimensions={0} | all-to-all | bytes 1310720 | tf_op jit(solution)/shard_map/all_to_all | solution.py:25
  86.0 0.1 shard_map.113
  86.1 2.3 %shard_map.114 = bf16[4,1056,128]{2,1,0:T(8,128)(2,1)} custom-call(s32[3]{0:T(128)S(1)} %pad_add_fusion.c_ref.at_ref, bf16[4,4,64,256]{3,2,1,0:T(8,128)(2,1)S(1)} %get-tuple-element.34.own_ref, bf16[4,4,64,256]{3,2,1,0:T(8,128)(2,1)S(1)} %collective-permute-done.other_ref, bf16[512,512]{1,0:T(8,128)(2,1)S(1)} %get-tuple-element.40.grads_ref, ...), custom_call_target="tpu_custom_call" | custom-call | tf_op jit(solution)/shard_map/pallas_call | solution.py:21
  88.4 3.5 %all-to-all-start.3 = ((bf16[4,1056,128]{2,1,0:T(8,128)(2,1)}), bf16[4,1056,128]{2,1,0:T(8,128)(2,1)S(1)}, u32[]{:S(2)}, u32[]{:S(2)}) async-start(bf16[4,1056,128]{2,1,0:T(8,128)(2,1)} %shard_map.114), calls=%async_computation.3 | async-start | bytes 2162688 | tf_op jit(solution)/shard_map/all_to_all | solution.py:25
  91.9 1.3 shard_map.116
  93.3 2.3 %collective-permute-start.1 = (bf16[4,4,64,256]{3,2,1,0:T(8,128)(2,1)S(1)}, bf16[4,4,64,256]{3,2,1,0:T(8,128)(2,1)S(1)}, u32[]{:S(2)}, u32[]{:S(2)}) collective-permute-start(bf16[4,4,64,256]{3,2,1,0:T(8,128)(2,1)S(1)} %get-tuple-element.45), channel_id=1, source_target_pairs={{0,16},{16,0},{1,17},{17,1},{2,18},{18,2},{3,19},{19,3},{4,20},{20... | collective-permute-start | bytes 1572872 | tf_op jit(solution)/shard_map/ppermute | solution.py:283
  95.6 1.5 %collective-permute-done.1.other_ref = bf16[4,4,64,256]{3,2,1,0:T(8,128)(2,1)S(1)} collective-permute-done((bf16[4,4,64,256]{3,2,1,0:T(8,128)(2,1)S(1)}, bf16[4,4,64,256]{3,2,1,0:T(8,128)(2,1)S(1)}, u32[]{:S(2)}, u32[]{:S(2)}) %collective-permute-start.1) | collective-permute-done | bytes 524320 | tf_op jit(solution)/shard_map/ppermute | solution.py:283
  97.1 0.1 shard_map.117
  97.2 1.9 %collective-permute-start.2 = (bf16[2,4,64,256]{3,2,1,0:T(8,128)(2,1)S(1)}, bf16[2,4,64,256]{3,2,1,0:T(8,128)(2,1)S(1)}, u32[]{:S(2)}, u32[]{:S(2)}) collective-permute-start(bf16[2,4,64,256]{3,2,1,0:T(8,128)(2,1)S(1)} %get-tuple-element.46), channel_id=1, source_target_pairs={{0,32},{32,0},{64,96},{96,64},{1,33},{33,1},{65,97},{97,65},{2,34}... | collective-permute-start | bytes 786440 | tf_op jit(solution)/shard_map/ppermute | solution.py:285
  99.1 7.9 %all-to-all-done.3.parts_ref = bf16[4,1056,128]{2,1,0:T(8,128)(2,1)S(1)} async-done(((bf16[4,1056,128]{2,1,0:T(8,128)(2,1)}), bf16[4,1056,128]{2,1,0:T(8,128)(2,1)S(1)}, u32[]{:S(2)}, u32[]{:S(2)}) %all-to-all-start.3) | async-done | bytes 1081376 | tf_op jit(solution)/shard_map/all_to_all | solution.py:25
  107.1 0.8 shard_map.115
  107.9 0.0 collective-permute-done.2.other_ref
  107.9 12.1 %all-to-all-start.4 = ((bf16[4,272,128]{2,1,0:T(8,128)(2,1)}), bf16[4,272,128]{2,1,0:T(8,128)(2,1)S(1)}, u32[]{:S(2)}, u32[]{:S(2)}) async-start(bf16[4,272,128]{2,1,0:T(8,128)(2,1)} %shard_map.115), calls=%async_computation.4 | async-start | bytes 557056 | tf_op jit(solution)/shard_map/all_to_all | solution.py:25
  120.1 2.2 %collective-permute-start.3 = (bf16[4,64,256]{2,1,0:T(8,128)(2,1)S(1)}, bf16[4,64,256]{2,1,0:T(8,128)(2,1)S(1)}, u32[]{:S(2)}, u32[]{:S(2)}) collective-permute-start(bf16[4,64,256]{2,1,0:T(8,128)(2,1)S(1)} %get-tuple-element.51), channel_id=1, source_target_pairs={{0,64},{32,96},{64,0},{96,32},{1,65},{33,97},{65,1},{97,33},{2,66}... | collective-permute-start | bytes 393224 | tf_op jit(solution)/shard_map/ppermute | solution.py:289
  122.3 5.0 %collective-permute-done.3.other_ref = bf16[4,64,256]{2,1,0:T(8,128)(2,1)S(1)} collective-permute-done((bf16[4,64,256]{2,1,0:T(8,128)(2,1)S(1)}, bf16[4,64,256]{2,1,0:T(8,128)(2,1)S(1)}, u32[]{:S(2)}, u32[]{:S(2)}) %collective-permute-start.3) | collective-permute-done | bytes 131104 | tf_op jit(solution)/shard_map/ppermute | solution.py:289
  127.3 3.8 %collective-permute-start.4 = (bf16[64,256]{1,0:T(8,128)(2,1)S(1)}, bf16[64,256]{1,0:T(8,128)(2,1)S(1)}, u32[]{:S(2)}, u32[]{:S(2)}) collective-permute-start(bf16[64,256]{1,0:T(8,128)(2,1)S(1)} %get-tuple-element.52), channel_id=1, source_target_pairs={{0,2},{1,3},{2,0},{3,1},{4,6},{5,7},{6,4},{7,5},{8,10},{9,11},{10,... | collective-permute-start | bytes 98312 | tf_op jit(solution)/shard_map/ppermute | solution.py:291
  131.1 2.2 %collective-permute-start.6 = (bf16[64,256]{1,0:T(8,128)(2,1)S(1)}, bf16[64,256]{1,0:T(8,128)(2,1)S(1)}, u32[]{:S(2)}, u32[]{:S(2)}) collective-permute-start(bf16[64,256]{1,0:T(8,128)(2,1)S(1)} %get-tuple-element.56), channel_id=1, source_target_pairs={{0,1},{1,2},{2,3},{3,0},{4,5},{5,6},{6,7},{7,4},{8,9},{9,10},{10,1... | collective-permute-start | bytes 98312 | tf_op jit(solution)/shard_map/ppermute | solution.py:291
  133.3 4.3 %collective-permute-start.7 = (bf16[64,256]{1,0:T(8,128)(2,1)S(1)}, bf16[64,256]{1,0:T(8,128)(2,1)S(1)}, u32[]{:S(2)}, u32[]{:S(2)}) collective-permute-start(bf16[64,256]{1,0:T(8,128)(2,1)S(1)} %get-tuple-element.57), channel_id=1, source_target_pairs={{0,3},{1,0},{2,1},{3,2},{4,7},{5,4},{6,5},{7,6},{8,11},{9,8},{10,9... | collective-permute-start | bytes 98312 | tf_op jit(solution)/shard_map/ppermute | solution.py:291
  137.6 0.0 collective-permute-done.4.refs_3_
  137.6 0.0 all-to-all-done.4.parts_ref
  137.7 0.7 shard_map.120
  138.3 5.4 %collective-permute-start.5 = (f32[16,128]{1,0:T(8,128)S(1)}, f32[16,128]{1,0:T(8,128)S(1)}, u32[]{:S(2)}, u32[]{:S(2)}) collective-permute-start(f32[16,128]{1,0:T(8,128)S(1)} %get-tuple-element.54.gain_ref), channel_id=1, source_target_pairs={{0,16},{16,0},{1,17},{17,1},{2,18},{18,2},{3,19},{19,3},{4,20},{20... | collective-permute-start | bytes 24584 | tf_op jit(solution)/shard_map/ppermute | solution.py:301
  143.7 0.0 collective-permute-done.6.refs_1_
  143.7 0.0 collective-permute-done.7.refs_2_
  143.7 0.8 collective-permute-done.5.other_ref
  144.5 1.2 shard_map.121
  (2 shorter events, 0.1 us)
Async XLA Ops:
  30.3 7.6 %collective-permute-start = (bf16[4,4,64,256]{3,2,1,0:T(8,128)(2,1)S(1)}, bf16[4,4,64,256]{3,2,1,0:T(8,128)(2,1)S(1)}, u32[]{:S(2)}, u32[]{:S(2)}) collective-permute-start(bf16[4,4,64,256]{3,2,1,0:T(8,128)(2,1)S(1)} %get-tuple-element.34.own_ref), channel_id=1, source_target_pairs={{0,16},{16,0},{1,17},{17,1},{2,18},{18,2},{3,19},{19,3},{4,20},{20... | collective-permute-start | bytes 1572872 | tf_op jit(solution)/shard_map/ppermute | solution.py:253
  37.9 24.0 %copy-start = (bf16[16,4096]{1,0:T(8,128)(2,1)S(1)}, bf16[16,4096]{1,0:T(8,128)(2,1)}, u32[]{:S(2)}) copy-start(bf16[16,4096]{1,0:T(8,128)(2,1)} %residual_ref.1) | copy-start | bytes 393220
  37.9 24.0 %copy-start.1 = (bf16[16,4096]{1,0:T(8,128)(2,1)S(1)}, bf16[16,4096]{1,0:T(8,128)(2,1)}, u32[]{:S(2)}) copy-start(bf16[16,4096]{1,0:T(8,128)(2,1)} %upstream_ref.1) | copy-start | bytes 393220
  37.9 24.0 %copy-start.2 = (bf16[16,4096]{1,0:T(8,128)(2,1)S(1)}, bf16[16,4096]{1,0:T(8,128)(2,1)}, u32[]{:S(2)}) copy-start(bf16[16,4096]{1,0:T(8,128)(2,1)} %resid_grad_ref.1) | copy-start | bytes 393220
  38.0 24.0 %copy-start.3 = (f32[4096]{0:T(1024)S(1)}, f32[4096]{0:T(1024)}, u32[]{:S(2)}) copy-start(f32[4096]{0:T(1024)} %param.9) | copy-start | bytes 49156
  88.4 18.6 %all-to-all-start.3 = ((bf16[4,1056,128]{2,1,0:T(8,128)(2,1)}), bf16[4,1056,128]{2,1,0:T(8,128)(2,1)S(1)}, u32[]{:S(2)}, u32[]{:S(2)}) async-start(bf16[4,1056,128]{2,1,0:T(8,128)(2,1)} %shard_map.114), calls=%async_computation.3 | async-start | bytes 2162688 | tf_op jit(solution)/shard_map/all_to_all | solution.py:25
  93.3 3.8 %collective-permute-start.1 = (bf16[4,4,64,256]{3,2,1,0:T(8,128)(2,1)S(1)}, bf16[4,4,64,256]{3,2,1,0:T(8,128)(2,1)S(1)}, u32[]{:S(2)}, u32[]{:S(2)}) collective-permute-start(bf16[4,4,64,256]{3,2,1,0:T(8,128)(2,1)S(1)} %get-tuple-element.45), channel_id=1, source_target_pairs={{0,16},{16,0},{1,17},{17,1},{2,18},{18,2},{3,19},{19,3},{4,20},{20... | collective-permute-start | bytes 1572872 | tf_op jit(solution)/shard_map/ppermute | solution.py:283
  97.2 10.7 %collective-permute-start.2 = (bf16[2,4,64,256]{3,2,1,0:T(8,128)(2,1)S(1)}, bf16[2,4,64,256]{3,2,1,0:T(8,128)(2,1)S(1)}, u32[]{:S(2)}, u32[]{:S(2)}) collective-permute-start(bf16[2,4,64,256]{3,2,1,0:T(8,128)(2,1)S(1)} %get-tuple-element.46), channel_id=1, source_target_pairs={{0,32},{32,0},{64,96},{96,64},{1,33},{33,1},{65,97},{97,65},{2,34}... | collective-permute-start | bytes 786440 | tf_op jit(solution)/shard_map/ppermute | solution.py:285
  107.9 29.7 %all-to-all-start.4 = ((bf16[4,272,128]{2,1,0:T(8,128)(2,1)}), bf16[4,272,128]{2,1,0:T(8,128)(2,1)S(1)}, u32[]{:S(2)}, u32[]{:S(2)}) async-start(bf16[4,272,128]{2,1,0:T(8,128)(2,1)} %shard_map.115), calls=%async_computation.4 | async-start | bytes 557056 | tf_op jit(solution)/shard_map/all_to_all | solution.py:25
  120.1 7.2 %collective-permute-start.3 = (bf16[4,64,256]{2,1,0:T(8,128)(2,1)S(1)}, bf16[4,64,256]{2,1,0:T(8,128)(2,1)S(1)}, u32[]{:S(2)}, u32[]{:S(2)}) collective-permute-start(bf16[4,64,256]{2,1,0:T(8,128)(2,1)S(1)} %get-tuple-element.51), channel_id=1, source_target_pairs={{0,64},{32,96},{64,0},{96,32},{1,65},{33,97},{65,1},{97,33},{2,66}... | collective-permute-start | bytes 393224 | tf_op jit(solution)/shard_map/ppermute | solution.py:289
  127.3 10.3 %collective-permute-start.4 = (bf16[64,256]{1,0:T(8,128)(2,1)S(1)}, bf16[64,256]{1,0:T(8,128)(2,1)S(1)}, u32[]{:S(2)}, u32[]{:S(2)}) collective-permute-start(bf16[64,256]{1,0:T(8,128)(2,1)S(1)} %get-tuple-element.52), channel_id=1, source_target_pairs={{0,2},{1,3},{2,0},{3,1},{4,6},{5,7},{6,4},{7,5},{8,10},{9,11},{10,... | collective-permute-start | bytes 98312 | tf_op jit(solution)/shard_map/ppermute | solution.py:291
  131.1 12.6 %collective-permute-start.6 = (bf16[64,256]{1,0:T(8,128)(2,1)S(1)}, bf16[64,256]{1,0:T(8,128)(2,1)S(1)}, u32[]{:S(2)}, u32[]{:S(2)}) collective-permute-start(bf16[64,256]{1,0:T(8,128)(2,1)S(1)} %get-tuple-element.56), channel_id=1, source_target_pairs={{0,1},{1,2},{2,3},{3,0},{4,5},{5,6},{6,7},{7,4},{8,9},{9,10},{10,1... | collective-permute-start | bytes 98312 | tf_op jit(solution)/shard_map/ppermute | solution.py:291
  133.3 10.4 %collective-permute-start.7 = (bf16[64,256]{1,0:T(8,128)(2,1)S(1)}, bf16[64,256]{1,0:T(8,128)(2,1)S(1)}, u32[]{:S(2)}, u32[]{:S(2)}) collective-permute-start(bf16[64,256]{1,0:T(8,128)(2,1)S(1)} %get-tuple-element.57), channel_id=1, source_target_pairs={{0,3},{1,0},{2,1},{3,2},{4,7},{5,4},{6,5},{7,6},{8,11},{9,8},{10,9... | collective-permute-start | bytes 98312 | tf_op jit(solution)/shard_map/ppermute | solution.py:291
  138.3 6.2 %collective-permute-start.5 = (f32[16,128]{1,0:T(8,128)S(1)}, f32[16,128]{1,0:T(8,128)S(1)}, u32[]{:S(2)}, u32[]{:S(2)}) collective-permute-start(f32[16,128]{1,0:T(8,128)S(1)} %get-tuple-element.54.gain_ref), channel_id=1, source_target_pairs={{0,16},{16,0},{1,17},{17,1},{2,18},{18,2},{3,19},{19,3},{4,20},{20... | collective-permute-start | bytes 24584 | tf_op jit(solution)/shard_map/ppermute | solution.py:301

commit v5 on v4

--- a/solution.py
+++ b/solution.py
@@ -109,7 +109,7 @@
 
 def norm_kernel(
     parts_ref, residual_ref, gain_ref, upstream_ref, resid_grad_ref,
-    normed_ref, stream_ref, grad_ref, cols_ref, projected_ref,
+    normed_ref, stream_ref, grad_ref, cols_ref, projected_ref, rows_ref,
 ):
     for c in range(2):
         for y in range(4):
@@ -135,11 +135,11 @@
     grad = (resid_grad_ref[...].astype(F32) + inv_rms * (scaled - unit_rows * inner)).astype(BF16)
     grad_ref[...] = grad
     for k in range(32):
-        rows = gain_grad[:, k * 128 : k * 128 + 128].astype(BF16)
-        rows = jnp.broadcast_to(rows[None], (4, 1, 128))
-        for z in range(4):
-            to = (z * 2 + k % 2) * 4
-            cols_ref[to : to + 4, 64 + k // 2 : 65 + k // 2] = rows
+        at = k % 2 * 16 + k // 2
+        rows_ref[at : at + 1] = gain_grad[:, k * 128 : k * 128 + 128]
+    for to in range(32):
+        at = to // 4 % 2 * 16
+        cols_ref[to, 64:] = rows_ref[at : at + 16].astype(BF16)
     for c in range(2):
         for y in range(4):
             for h in range(4):
@@ -162,20 +162,19 @@
     gain = gain_ref[...]
     upper = gain.astype(BF16)
     lower = (gain - upper.astype(F32)).astype(BF16)
-    for x in range(4):
-        total = jnp.zeros((256, 512), F32)
-        for att_ref, core in ((own_ref, c), (other_ref, 1 - c)):
-            total += lax.dot_general(
-                att_ref[:, x].reshape(256, 256),
-                grads_ref[pl.ds(pl.multiple_of(core * 256, 256), 256)],
-                (((0,), (0,)), ((), ())),
-                preferred_element_type=F32,
-            )
-        total = total.astype(BF16)
-        for h in range(4):
-            out_ref[x, h * 256 : h * 256 + 256] = total[:, h * 128 : h * 128 + 128]
-        out_ref[x, 1024:1040] = upper
-        out_ref[x, 1040:] = lower
+    total = jnp.zeros((256, 512), F32)
+    for att_ref, core in ((own_ref, c), (other_ref, 1 - c)):
+        total += lax.dot_general(
+            att_ref[:, pl.program_id(0)].reshape(256, 256),
+            grads_ref[pl.ds(pl.multiple_of(core * 256, 256), 256)],
+            (((0,), (0,)), ((), ())),
+            preferred_element_type=F32,
+        )
+    total = total.astype(BF16)
+    for h in range(4):
+        out_ref[0, h * 256 : h * 256 + 256] = total[:, h * 128 : h * 128 + 128]
+    out_ref[0, 1024:1040] = upper
+    out_ref[0, 1040:] = lower
 
 
 def weight_x_kernel(parts_ref, out_ref):
@@ -187,12 +186,15 @@
         out_ref[h, 256:] = (total[1024:1040] + total[1040:]).astype(BF16)
 
 
-def weight_zh_kernel(parts_ref, weight_ref, gain_ref):
-    total = parts_ref[0].astype(F32)
+def weight_zh_kernel(parts_ref, weight_ref):
+    total = parts_ref[0, :256].astype(F32)
     for k in range(1, 4):
-        total += parts_ref[k].astype(F32)
-    weight_ref[...] = total[:256]
-    gain_ref[...] = total[256:]
+        total += parts_ref[k, :256].astype(F32)
+    weight_ref[...] = total
+
+
+def gain_zh_kernel(parts_ref, gain_ref):
+    gain_ref[...] = jnp.sum(parts_ref[:, 256:].astype(F32), axis=0)
 
 
 def place(there, here):
@@ -259,7 +261,7 @@
         norm_kernel,
         out_shape=(shape((16, 4096)),) * 3 + (shape((32, 80, 128)),),
         in_specs=[WHOLE] * 5,
-        scratch_shapes=[pltpu.VMEM((16, 4096), F32)],
+        scratch_shapes=[pltpu.VMEM((16, 4096), F32), pltpu.VMEM((32, 128), F32)],
         compiler_params=PARAMS,
     )(parts, residual, norm_gain.reshape(1, 4096), grad_normed, grad_resid)
 
@@ -267,7 +269,14 @@
         unpack_kernel, (shape((512, 512)), shape((16, 128), F32)), a2a(cols, ("zl", "c", "y"))
     )
 
-    blocks = call(weight_kernel, shape((4, 1056, 128)), at, own, other, grads, gain)
+    blocks = pl.pallas_call(
+        weight_kernel,
+        grid=(4,),
+        out_shape=shape((4, 1056, 128)),
+        in_specs=[SCALAR] + [WHOLE] * 4,
+        out_specs=pl.BlockSpec((1, 1056, 128), lambda x: (x, 0, 0)),
+        compiler_params=PARAMS,
+    )(at, own, other, grads, gain)
     blocks, weight = lax.optimization_barrier((blocks, weight))
     by_zh = call(weight_x_kernel, shape((4, 272, 128)), a2a(blocks, "x"))
 
@@ -290,9 +299,8 @@
     back = call(add_last_kernel, (shape((64, 256)),) * 4, stay, far)
     moved = [lax.ppermute(back[k], "x", ring(k)) for k in (1, 3, 2)]
     parts, moved[2] = lax.optimization_barrier((parts, moved[2]))
-    weight_grad, gain = call(
-        weight_zh_kernel, (shape((256, 128), F32), shape((16, 128), F32)), parts
-    )
+    gain = call(gain_zh_kernel, shape((16, 128), F32), parts)
+    weight_grad = call(weight_zh_kernel, shape((256, 128), F32), parts)
     attn_grad, gain_grad = call(
         join_kernel,
         (shape((4, 4, 16, 256)), shape((32, 128), F32)),

time: 146 us -> 146 us (level)
  the two profiles are of different devices: /device:TPU:1 before, /device:TPU:6 now
where the time goes in v5:
time: 146 us; the launch traced here: 144 us
  blocking collectives  74 us (51%)
  starting transfers between devices  38.7 us (27%)
  waiting for transfers between devices  18.1 us (12%)
  Pallas kernels  12.1 us (8%)
    all_to_all x3, blocking collectives, a2a(): return lax.all_to_all(value, axes, 0, 0, tiled=True)  74 us
    all_to_all x2, starting transfers between devices, a2a(): return lax.all_to_all(value, axes, 0, 0, tiled=True)  17.9 us
    ppermute x3, starting transfers between devices, local(): moved = [lax.ppermute(back[k], 'x', ring(k)) for k in (1, 3, 2)]  9.27 us
    all_to_all x2, waiting for transfers between devices, a2a(): return lax.all_to_all(value, axes, 0, 0, tiled=True)  6.61 us
    pallas_call x11, Pallas kernels, call(): pl.pallas_call(kernel, out_shape=out_shape, in_specs=specs, compiler_para...  5.68 us
    ppermute x1, waiting for transfers between devices, local(): far = lax.ppermute(go, 'y', apart(2))  4.74 us
    ppermute x1, starting transfers between devices, local(): far = lax.ppermute(go, 'y', apart(2))  3.61 us
    pallas_call x1, Pallas kernels, local(): pl.pallas_call(weight_kernel, grid=(4,), out_shape=shape((4, 1056, 128)),...  2.99 us
  transfers between devices with their start and end apart: 10, of which 6 were waited for; matrix products, arithmetic and copies ran while one was open for 0% of the time, Pallas kernels for 2%

profile of v5, /device:TPU:6, one launch (start us, length us, event | category | flops | bytes accessed | tf_op | source)
XLA Modules:
  0.0 143.8 jit_solution(16551952834142298234)
XLA Ops:
  0.6 2.3 %shard_map.109 = bf16[16,192,256]{2,1,0:T(8,128)(2,1)} custom-call(bf16[256,256]{1,0:T(8,128)(2,1)} %att_hbm_ref.1, bf16[256,4096]{1,0:T(8,128)(2,1)} %weight_ref.1), custom_call_target="tpu_custom_call" | custom-call | tf_op jit(solution)/shard_map/pallas_call | solution.py:65
  3.0 27.6 %all_to_all.25 = bf16[16,192,256]{2,1,0:T(8,128)(2,1)S(1)} all-to-all(bf16[16,192,256]{2,1,0:T(8,128)(2,1)} %shard_map.109), channel_id=1, replica_groups=mesh['zh'=4,'y'=4,'c'=2,'zl'=4,'x'=4] {'y','x'}, dimensions={0} | all-to-all | bytes 3145728 | tf_op jit(solution)/shard_map/all_to_all | solution.py:25
  30.5 0.1 shard_map.110
  30.6 1.9 %collective-permute-start = (bf16[4,4,64,256]{3,2,1,0:T(8,128)(2,1)S(1)}, bf16[4,4,64,256]{3,2,1,0:T(8,128)(2,1)S(1)}, u32[]{:S(2)}, u32[]{:S(2)}) collective-permute-start(bf16[4,4,64,256]{3,2,1,0:T(8,128)(2,1)S(1)} %get-tuple-element.32.own_ref), channel_id=1, source_target_pairs={{0,16},{16,0},{1,17},{17,1},{2,18},{18,2},{3,19},{19,3},{4,20},{20... | collective-permute-start | bytes 1572872 | tf_op jit(solution)/shard_map/ppermute | solution.py:255
  32.6 0.1 pad_add_fusion.c_ref.at_ref
  32.6 1.8 %collective-permute-done.other_ref = bf16[4,4,64,256]{3,2,1,0:T(8,128)(2,1)S(1)} collective-permute-done((bf16[4,4,64,256]{3,2,1,0:T(8,128)(2,1)S(1)}, bf16[4,4,64,256]{3,2,1,0:T(8,128)(2,1)S(1)}, u32[]{:S(2)}, u32[]{:S(2)}) %collective-permute-start) | collective-permute-done | bytes 524320 | tf_op jit(solution)/shard_map/ppermute | solution.py:255
  34.4 0.0 copy-start
  34.4 0.0 copy-start.1
  34.4 0.0 copy-start.2
  34.4 0.0 copy-start.3
  34.5 1.2 shard_map.111
  35.7 23.6 %all_to_all.26.parts_ref = bf16[32,16,512]{2,1,0:T(8,128)(2,1)S(1)} all-to-all(bf16[32,16,512]{2,1,0:T(8,128)(2,1)S(1)} %shard_map.111), channel_id=1, replica_groups=mesh['zh'=4,'y'=4,'c'=2,'zl'=4,'x'=4] {'zl','c','y'}, dimensions={0} | all-to-all | bytes 1048576 | tf_op jit(solution)/shard_map/all_to_all | solution.py:25
  59.3 0.0 copy-done
  59.3 0.0 copy-done.1
  59.3 0.0 copy-done.2
  59.3 0.0 copy-done.3
  59.3 1.1 shard_map.112
  60.4 22.9 %all_to_all.27.parts_ref = bf16[32,80,128]{2,1,0:T(8,128)(2,1)S(1)} all-to-all(bf16[32,80,128]{2,1,0:T(8,128)(2,1)S(1)} %get-tuple-element.37), channel_id=1, replica_groups=mesh['zh'=4,'y'=4,'c'=2,'zl'=4,'x'=4] {'zl','c','y'}, dimensions={0} | all-to-all | bytes 1310720 | tf_op jit(solution)/shard_map/all_to_all | solution.py:25
  83.3 0.1 shard_map.113
  83.4 3.0 %shard_map.114 = bf16[4,1056,128]{2,1,0:T(8,128)(2,1)} custom-call(s32[3]{0:T(128)S(1)} %pad_add_fusion.c_ref.at_ref, bf16[4,4,64,256]{3,2,1,0:T(8,128)(2,1)S(1)} %get-tuple-element.32.own_ref, bf16[4,4,64,256]{3,2,1,0:T(8,128)(2,1)S(1)} %collective-permute-done.other_ref, bf16[512,512]{1,0:T(8,128)(2,1)S(1)} %get-tuple-element.38.grads_ref, ...), custom_call_target="tpu_custom_call" | custom-call | tf_op jit(solution)/shard_map/pallas_call | solution.py:272
  86.4 5.6 %all-to-all-start.3 = ((bf16[4,1056,128]{2,1,0:T(8,128)(2,1)}), bf16[4,1056,128]{2,1,0:T(8,128)(2,1)S(1)}, u32[]{:S(2)}, u32[]{:S(2)}) async-start(bf16[4,1056,128]{2,1,0:T(8,128)(2,1)} %shard_map.114), calls=%async_computation.3 | async-start | bytes 2162688 | tf_op jit(solution)/shard_map/all_to_all | solution.py:25
  91.9 1.3 shard_map.116
  93.3 1.9 %collective-permute-start.1 = (bf16[4,4,64,256]{3,2,1,0:T(8,128)(2,1)S(1)}, bf16[4,4,64,256]{3,2,1,0:T(8,128)(2,1)S(1)}, u32[]{:S(2)}, u32[]{:S(2)}) collective-permute-start(bf16[4,4,64,256]{3,2,1,0:T(8,128)(2,1)S(1)} %get-tuple-element.43), channel_id=1, source_target_pairs={{0,16},{16,0},{1,17},{17,1},{2,18},{18,2},{3,19},{19,3},{4,20},{20... | collective-permute-start | bytes 1572872 | tf_op jit(solution)/shard_map/ppermute | solution.py:292
  95.2 1.9 %collective-permute-done.1.other_ref = bf16[4,4,64,256]{3,2,1,0:T(8,128)(2,1)S(1)} collective-permute-done((bf16[4,4,64,256]{3,2,1,0:T(8,128)(2,1)S(1)}, bf16[4,4,64,256]{3,2,1,0:T(8,128)(2,1)S(1)}, u32[]{:S(2)}, u32[]{:S(2)}) %collective-permute-start.1) | collective-permute-done | bytes 524320 | tf_op jit(solution)/shard_map/ppermute | solution.py:292
  97.1 0.1 shard_map.117
  97.2 2.1 %collective-permute-start.2 = (bf16[2,4,64,256]{3,2,1,0:T(8,128)(2,1)S(1)}, bf16[2,4,64,256]{3,2,1,0:T(8,128)(2,1)S(1)}, u32[]{:S(2)}, u32[]{:S(2)}) collective-permute-start(bf16[2,4,64,256]{3,2,1,0:T(8,128)(2,1)S(1)} %get-tuple-element.44), channel_id=1, source_target_pairs={{0,32},{32,0},{64,96},{96,64},{1,33},{33,1},{65,97},{97,65},{2,34}... | collective-permute-start | bytes 786440 | tf_op jit(solution)/shard_map/ppermute | solution.py:294
  99.3 6.6 %all-to-all-done.3.parts_ref = bf16[4,1056,128]{2,1,0:T(8,128)(2,1)S(1)} async-done(((bf16[4,1056,128]{2,1,0:T(8,128)(2,1)}), bf16[4,1056,128]{2,1,0:T(8,128)(2,1)S(1)}, u32[]{:S(2)}, u32[]{:S(2)}) %all-to-all-start.3) | async-done | bytes 1081376 | tf_op jit(solution)/shard_map/all_to_all | solution.py:25
  105.9 0.8 shard_map.115
  106.7 0.7 collective-permute-done.2.other_ref
  107.4 12.4 %all-to-all-start.4 = ((bf16[4,272,128]{2,1,0:T(8,128)(2,1)}), bf16[4,272,128]{2,1,0:T(8,128)(2,1)S(1)}, u32[]{:S(2)}, u32[]{:S(2)}) async-start(bf16[4,272,128]{2,1,0:T(8,128)(2,1)} %shard_map.115), calls=%async_computation.4 | async-start | bytes 557056 | tf_op jit(solution)/shard_map/all_to_all | solution.py:25
  119.8 3.6 %collective-permute-start.3 = (bf16[4,64,256]{2,1,0:T(8,128)(2,1)S(1)}, bf16[4,64,256]{2,1,0:T(8,128)(2,1)S(1)}, u32[]{:S(2)}, u32[]{:S(2)}) collective-permute-start(bf16[4,64,256]{2,1,0:T(8,128)(2,1)S(1)} %get-tuple-element.49), channel_id=1, source_target_pairs={{0,64},{32,96},{64,0},{96,32},{1,65},{33,97},{65,1},{97,33},{2,66}... | collective-permute-start | bytes 393224 | tf_op jit(solution)/shard_map/ppermute | solution.py:298
  123.4 4.7 %collective-permute-done.3.other_ref = bf16[4,64,256]{2,1,0:T(8,128)(2,1)S(1)} collective-permute-done((bf16[4,64,256]{2,1,0:T(8,128)(2,1)S(1)}, bf16[4,64,256]{2,1,0:T(8,128)(2,1)S(1)}, u32[]{:S(2)}, u32[]{:S(2)}) %collective-permute-start.3) | collective-permute-done | bytes 131104 | tf_op jit(solution)/shard_map/ppermute | solution.py:298
  128.2 3.4 %collective-permute-start.4 = (bf16[64,256]{1,0:T(8,128)(2,1)S(1)}, bf16[64,256]{1,0:T(8,128)(2,1)S(1)}, u32[]{:S(2)}, u32[]{:S(2)}) collective-permute-start(bf16[64,256]{1,0:T(8,128)(2,1)S(1)} %get-tuple-element.50), channel_id=1, source_target_pairs={{0,2},{1,3},{2,0},{3,1},{4,6},{5,7},{6,4},{7,5},{8,10},{9,11},{10,... | collective-permute-start | bytes 98312 | tf_op jit(solution)/shard_map/ppermute | solution.py:300
  131.6 4.0 %collective-permute-start.6 = (bf16[64,256]{1,0:T(8,128)(2,1)S(1)}, bf16[64,256]{1,0:T(8,128)(2,1)S(1)}, u32[]{:S(2)}, u32[]{:S(2)}) collective-permute-start(bf16[64,256]{1,0:T(8,128)(2,1)S(1)} %get-tuple-element.53), channel_id=1, source_target_pairs={{0,1},{1,2},{2,3},{3,0},{4,5},{5,6},{6,7},{7,4},{8,9},{9,10},{10,1... | collective-permute-start | bytes 98312 | tf_op jit(solution)/shard_map/ppermute | solution.py:300
  135.6 1.9 %collective-permute-start.7 = (bf16[64,256]{1,0:T(8,128)(2,1)S(1)}, bf16[64,256]{1,0:T(8,128)(2,1)S(1)}, u32[]{:S(2)}, u32[]{:S(2)}) collective-permute-start(bf16[64,256]{1,0:T(8,128)(2,1)S(1)} %get-tuple-element.54), channel_id=1, source_target_pairs={{0,3},{1,0},{2,1},{3,2},{4,7},{5,4},{6,5},{7,6},{8,11},{9,8},{10,9... | collective-permute-start | bytes 98312 | tf_op jit(solution)/shard_map/ppermute | solution.py:300
  137.5 0.0 collective-permute-done.4.refs_3_
  137.5 0.0 all-to-all-done.4.parts_ref
  137.5 1.9 %collective-permute-start.5 = (f32[16,128]{1,0:T(8,128)S(1)}, f32[16,128]{1,0:T(8,128)S(1)}, u32[]{:S(2)}, u32[]{:S(2)}) collective-permute-start(f32[16,128]{1,0:T(8,128)S(1)} %shard_map.120.gain_ref), channel_id=1, source_target_pairs={{0,16},{16,0},{1,17},{17,1},{2,18},{18,2},{3,19},{19,3},{4,20},{20... | collective-permute-start | bytes 24584 | tf_op jit(solution)/shard_map/ppermute | solution.py:309
  139.5 0.7 shard_map.122
  140.2 0.0 collective-permute-done.6.refs_1_
  140.2 2.4 %collective-permute-done.7.refs_2_ = bf16[64,256]{1,0:T(8,128)(2,1)S(1)} collective-permute-done((bf16[64,256]{1,0:T(8,128)(2,1)S(1)}, bf16[64,256]{1,0:T(8,128)(2,1)S(1)}, u32[]{:S(2)}, u32[]{:S(2)}) %collective-permute-start.7) | collective-permute-done | bytes 32800 | tf_op jit(solution)/shard_map/ppermute | solution.py:300
  142.6 0.0 collective-permute-done.5.other_ref
  142.6 1.2 shard_map.121
  (3 shorter events, 0.1 us)
Async XLA Ops:
  30.6 3.8 %collective-permute-start = (bf16[4,4,64,256]{3,2,1,0:T(8,128)(2,1)S(1)}, bf16[4,4,64,256]{3,2,1,0:T(8,128)(2,1)S(1)}, u32[]{:S(2)}, u32[]{:S(2)}) collective-permute-start(bf16[4,4,64,256]{3,2,1,0:T(8,128)(2,1)S(1)} %get-tuple-element.32.own_ref), channel_id=1, source_target_pairs={{0,16},{16,0},{1,17},{17,1},{2,18},{18,2},{3,19},{19,3},{4,20},{20... | collective-permute-start | bytes 1572872 | tf_op jit(solution)/shard_map/ppermute | solution.py:255
  34.4 24.9 %copy-start = (bf16[16,4096]{1,0:T(8,128)(2,1)S(1)}, bf16[16,4096]{1,0:T(8,128)(2,1)}, u32[]{:S(2)}) copy-start(bf16[16,4096]{1,0:T(8,128)(2,1)} %residual_ref.1) | copy-start | bytes 393220
  34.4 24.9 %copy-start.1 = (bf16[16,4096]{1,0:T(8,128)(2,1)S(1)}, bf16[16,4096]{1,0:T(8,128)(2,1)}, u32[]{:S(2)}) copy-start(bf16[16,4096]{1,0:T(8,128)(2,1)} %upstream_ref.1) | copy-start | bytes 393220
  34.4 24.9 %copy-start.2 = (bf16[16,4096]{1,0:T(8,128)(2,1)S(1)}, bf16[16,4096]{1,0:T(8,128)(2,1)}, u32[]{:S(2)}) copy-start(bf16[16,4096]{1,0:T(8,128)(2,1)} %resid_grad_ref.1) | copy-start | bytes 393220
  34.4 24.9 %copy-start.3 = (f32[4096]{0:T(1024)S(1)}, f32[4096]{0:T(1024)}, u32[]{:S(2)}) copy-start(f32[4096]{0:T(1024)} %param.9) | copy-start | bytes 49156
  86.4 19.5 %all-to-all-start.3 = ((bf16[4,1056,128]{2,1,0:T(8,128)(2,1)}), bf16[4,1056,128]{2,1,0:T(8,128)(2,1)S(1)}, u32[]{:S(2)}, u32[]{:S(2)}) async-start(bf16[4,1056,128]{2,1,0:T(8,128)(2,1)} %shard_map.114), calls=%async_computation.3 | async-start | bytes 2162688 | tf_op jit(solution)/shard_map/all_to_all | solution.py:25
  93.3 3.8 %collective-permute-start.1 = (bf16[4,4,64,256]{3,2,1,0:T(8,128)(2,1)S(1)}, bf16[4,4,64,256]{3,2,1,0:T(8,128)(2,1)S(1)}, u32[]{:S(2)}, u32[]{:S(2)}) collective-permute-start(bf16[4,4,64,256]{3,2,1,0:T(8,128)(2,1)S(1)} %get-tuple-element.43), channel_id=1, source_target_pairs={{0,16},{16,0},{1,17},{17,1},{2,18},{18,2},{3,19},{19,3},{4,20},{20... | collective-permute-start | bytes 1572872 | tf_op jit(solution)/shard_map/ppermute | solution.py:292
  97.2 10.2 %collective-permute-start.2 = (bf16[2,4,64,256]{3,2,1,0:T(8,128)(2,1)S(1)}, bf16[2,4,64,256]{3,2,1,0:T(8,128)(2,1)S(1)}, u32[]{:S(2)}, u32[]{:S(2)}) collective-permute-start(bf16[2,4,64,256]{3,2,1,0:T(8,128)(2,1)S(1)} %get-tuple-element.44), channel_id=1, source_target_pairs={{0,32},{32,0},{64,96},{96,64},{1,33},{33,1},{65,97},{97,65},{2,34}... | collective-permute-start | bytes 786440 | tf_op jit(solution)/shard_map/ppermute | solution.py:294
  107.4 30.1 %all-to-all-start.4 = ((bf16[4,272,128]{2,1,0:T(8,128)(2,1)}), bf16[4,272,128]{2,1,0:T(8,128)(2,1)S(1)}, u32[]{:S(2)}, u32[]{:S(2)}) async-start(bf16[4,272,128]{2,1,0:T(8,128)(2,1)} %shard_map.115), calls=%async_computation.4 | async-start | bytes 557056 | tf_op jit(solution)/shard_map/all_to_all | solution.py:25
  119.8 8.4 %collective-permute-start.3 = (bf16[4,64,256]{2,1,0:T(8,128)(2,1)S(1)}, bf16[4,64,256]{2,1,0:T(8,128)(2,1)S(1)}, u32[]{:S(2)}, u32[]{:S(2)}) collective-permute-start(bf16[4,64,256]{2,1,0:T(8,128)(2,1)S(1)} %get-tuple-element.49), channel_id=1, source_target_pairs={{0,64},{32,96},{64,0},{96,32},{1,65},{33,97},{65,1},{97,33},{2,66}... | collective-permute-start | bytes 393224 | tf_op jit(solution)/shard_map/ppermute | solution.py:298
  128.2 9.3 %collective-permute-start.4 = (bf16[64,256]{1,0:T(8,128)(2,1)S(1)}, bf16[64,256]{1,0:T(8,128)(2,1)S(1)}, u32[]{:S(2)}, u32[]{:S(2)}) collective-permute-start(bf16[64,256]{1,0:T(8,128)(2,1)S(1)} %get-tuple-element.50), channel_id=1, source_target_pairs={{0,2},{1,3},{2,0},{3,1},{4,6},{5,7},{6,4},{7,5},{8,10},{9,11},{10,... | collective-permute-start | bytes 98312 | tf_op jit(solution)/shard_map/ppermute | solution.py:300
  131.6 8.6 %collective-permute-start.6 = (bf16[64,256]{1,0:T(8,128)(2,1)S(1)}, bf16[64,256]{1,0:T(8,128)(2,1)S(1)}, u32[]{:S(2)}, u32[]{:S(2)}) collective-permute-start(bf16[64,256]{1,0:T(8,128)(2,1)S(1)} %get-tuple-element.53), channel_id=1, source_target_pairs={{0,1},{1,2},{2,3},{3,0},{4,5},{5,6},{6,7},{7,4},{8,9},{9,10},{10,1... | collective-permute-start | bytes 98312 | tf_op jit(solution)/shard_map/ppermute | solution.py:300
  135.6 7.0 %collective-permute-start.7 = (bf16[64,256]{1,0:T(8,128)(2,1)S(1)}, bf16[64,256]{1,0:T(8,128)(2,1)S(1)}, u32[]{:S(2)}, u32[]{:S(2)}) collective-permute-start(bf16[64,256]{1,0:T(8,128)(2,1)S(1)} %get-tuple-element.54), channel_id=1, source_target_pairs={{0,3},{1,0},{2,1},{3,2},{4,7},{5,4},{6,5},{7,6},{8,11},{9,8},{10,9... | collective-permute-start | bytes 98312 | tf_op jit(solution)/shard_map/ppermute | solution.py:300
  137.5 5.1 %collective-permute-start.5 = (f32[16,128]{1,0:T(8,128)S(1)}, f32[16,128]{1,0:T(8,128)S(1)}, u32[]{:S(2)}, u32[]{:S(2)}) collective-permute-start(f32[16,128]{1,0:T(8,128)S(1)} %shard_map.120.gain_ref), channel_id=1, source_target_pairs={{0,16},{16,0},{1,17},{17,1},{2,18},{18,2},{3,19},{19,3},{4,20},{20... | collective-permute-start | bytes 24584 | tf_op jit(solution)/shard_map/ppermute | solution.py:309
